TPU v7x, 1024 devices: a whole 8x8x8 slice. The times are simulated.
1024 devices in a mesh: gx: 16 (over z, core), gy: 64 (over x, y).
Axes of the slice: x: 8, y: 8, z: 8, core: 2. Of those that a mesh axis runs over, the one named last changes fastest.
Arguments:
- populations: float32 [19, 256, 256, 128], P(None, 'gx', 'gy'), as said below
- vert_base: int32 [3, 524288], P(None, ('gx', 'gy')), may hold values from 0 to 255, as said below
- vert_frac: float32 [3, 524288], P(None, ('gx', 'gy')), may hold values from 0 to 0.999
- edges: int32 [2, 1572864], P(None, ('gx', 'gy')), may hold values from 0 to 511, as said below
- stiffness: float32 [1572864], P(('gx', 'gy')), may hold values from 0.05 to 0.5
- rest: float32 [3, 1572864], P(None, ('gx', 'gy')), may hold values from -3 to 3
Outputs:
- fresh: float32 [19, 256, 256, 128], P(None, 'gx', 'gy')
- vertex_velocity: float32 [3, 524288], P(None, ('gx', 'gy'))
Inputs may be any that keep to these rules, and one draw needn't show every extreme that they name: `vert_base`: the first coordinate lies below 256, the second below 256, the third below 128. The vertices are in blocks of 512, block k belonging to the k-th device in the order gx then gy; a vertex's first coordinate lies in that device's 16 cells along x, its second in its 4 cells along y. Each run of 128 vertices of a block lies in a box of 4 x 4 x 4 cells, periodic in z. `edges`: edge e belongs to block e // 1536; its two entries are distinct indices within that block's 512 vertices, both in the same run of 128 vertices. `populations`: every entry lies between 0.6 and 1.4 times the lattice weight of its direction.
All inputs are finite; a program needn't handle non-finite values.
Results may differ from a plain program's by a relative error of at most 0.000078.
Values sent between devices are 32-bit elements; how exact they have to be, the bound alone decides.
No kernel may reach another device: no remote copies, remote signals or barrier semaphores. Data moves between devices by JAX's collectives and lax.ppermute only.
A program may use at most 32 MiB of HBM per device.

v0:
```python
import jax
import jax.numpy as jnp
from jax import lax
from jax.sharding import PartitionSpec as P

lattice_speeds = [
    (0, 0, 0),
    (1, 0, 0),
    (-1, 0, 0),
    (0, 1, 0),
    (0, -1, 0),
    (0, 0, 1),
    (0, 0, -1),
    (1, 1, 0),
    (-1, -1, 0),
    (1, -1, 0),
    (-1, 1, 0),
    (1, 0, 1),
    (-1, 0, -1),
    (1, 0, -1),
    (-1, 0, 1),
    (0, 1, 1),
    (0, -1, -1),
    (0, 1, -1),
    (0, -1, 1),
]
lattice_weights = [1.0 / 3.0] + [1.0 / 18.0] * 6 + [1.0 / 36.0] * 12
relax_time = 0.9


def with_halo(shard, sides, width):
    for axis, dim in sides:
        size, length = (lax.axis_size(axis), shard.shape[dim])
        up = [(i, (i + 1) % size) for i in range(size)]
        down = [(j, i) for i, j in up]
        last = lax.slice_in_dim(shard, length - width, length, axis=dim)
        initial = lax.slice_in_dim(shard, 0, width, axis=dim)
        before = lax.ppermute(last, axis, up)
        after = lax.ppermute(initial, axis, down)
        shard = jnp.concatenate([before, shard, after], axis=dim)
    return shard


def outer_weight(r):
    return (5.0 - 2.0 * r - jnp.sqrt(-7.0 + 12.0 * r - 4.0 * r * r)) / 8.0


def inner_weight(r):
    return (3.0 - 2.0 * r + jnp.sqrt(1.0 + 4.0 * r - 4.0 * r * r)) / 8.0


def kernel_weights(frac):
    return jnp.stack(
        [
            outer_weight(1.0 + frac),
            inner_weight(frac),
            inner_weight(1.0 - frac),
            outer_weight(2.0 - frac),
        ]
    )


def collide(popul, force):
    speeds = jnp.asarray(lattice_speeds, jnp.float32)
    weights = jnp.asarray(lattice_weights, jnp.float32)[:, None, None, None]
    high = lax.Precision.HIGHEST
    density = jnp.sum(popul, axis=0)
    moment = jnp.tensordot(speeds.T, popul, axes=1, precision=high)
    velocity = (moment + 0.5 * force) / density
    along = jnp.tensordot(speeds, velocity, axes=1, precision=high)
    square = jnp.sum(velocity * velocity, axis=0)
    balance = weights * density * (1.0 + 3.0 * along + 4.5 * along * along - 1.5 * square)
    push = jnp.tensordot(speeds, force, axes=1, precision=high)
    work = jnp.sum(velocity * force, axis=0)
    source = (1.0 - 0.5 / relax_time) * weights * (3.0 * (push - work) + 9.0 * along * push)
    post = popul - (popul - balance) / relax_time + source
    return (post, velocity)


def one_axis(kernel, start, extent, wrap):
    cells = jnp.arange(extent, dtype=jnp.int32)[:, None]
    total = jnp.zeros((extent, kernel.shape[1]), jnp.float32)
    for step in range(4):
        target = start + step
        if wrap:
            target = target % extent
        total = total + jnp.where(cells == target[None, :], kernel[step][None, :], 0.0)
    return total


def per_device(populations, vert_base, vert_frac, edges, stiffness, rest):
    width_x = populations.shape[1]
    width_y = populations.shape[2]
    depth = populations.shape[3]
    count = vert_base.shape[1]
    high = lax.Precision.HIGHEST
    position = vert_base.astype(jnp.float32) + vert_frac
    stretch = stiffness[None, :] * (position[:, edges[1]] - position[:, edges[0]] - rest)
    membrane = (
        jnp.zeros((3, count), jnp.float32)
        .at[:, edges[0]]
        .add(stretch)
        .at[:, edges[1]]
        .add(-stretch)
    )
    kernel = kernel_weights(vert_frac)
    anchor_x = lax.axis_index("gx") * width_x
    anchor_y = lax.axis_index("gy") * width_y
    along_x = one_axis(kernel[:, 0], vert_base[0] - anchor_x + 1, width_x + 4, False)
    along_y = one_axis(kernel[:, 1], vert_base[1] - anchor_y + 1, width_y + 4, False)
    along_z = one_axis(kernel[:, 2], vert_base[2] - 1, depth, True)
    plane = (along_x[:, None, :] * along_y[None, :, :]).reshape(
        (width_x + 4) * (width_y + 4), count
    )
    loaded = membrane[:, None, :] * along_z[None, :, :]
    spread = jnp.einsum("av,czv->caz", plane, loaded, precision=high).reshape(
        3, width_x + 4, width_y + 4, depth
    )
    strips = jnp.concatenate([spread[:, 0:2], spread[:, width_x + 2 : width_x + 4]], axis=1)
    landed = with_halo(strips, (("gx", 1),), 2)
    middle = spread[:, 2 : width_x + 2]
    middle = middle.at[:, 0:2].add(landed[:, 0:2]).at[:, width_x - 2 : width_x].add(landed[:, 6:8])
    strips = jnp.concatenate([middle[:, :, 0:2], middle[:, :, width_y + 2 : width_y + 4]], axis=2)
    landed = with_halo(strips, (("gy", 2),), 2)
    grid = middle[:, :, 2 : width_y + 2]
    grid = (
        grid.at[:, :, 0:2]
        .add(landed[:, :, 0:2])
        .at[:, :, width_y - 2 : width_y]
        .add(landed[:, :, 6:8])
    )
    post, velocity = collide(populations, grid)
    carried = list(range(19))
    beside_all = with_halo(post, (("gx", 1), ("gy", 2)), 1)
    velocity_ext = with_halo(velocity, (("gx", 1), ("gy", 2)), 2)
    rows = []
    for q in range(19):
        step_x, step_y, step_z = lattice_speeds[q]
        slot = carried.index(q)
        moved = beside_all[
            slot, 1 - step_x : 1 - step_x + width_x, 1 - step_y : 1 - step_y + width_y
        ]
        rows.append(jnp.roll(moved, step_z, axis=2))
    fresh = jnp.stack(rows)
    flat = velocity_ext.reshape(3, (width_x + 4) * (width_y + 4), depth)
    partial_value = jnp.einsum("av,caz->czv", plane, flat, precision=high)
    sampled = jnp.sum(partial_value * along_z[None, :, :], axis=1)
    return (fresh, sampled)


def solution(mesh):
    placed = (
        P(None, "gx", "gy", None),
        P(None, ("gx", "gy")),
        P(None, ("gx", "gy")),
        P(None, ("gx", "gy")),
        P(("gx", "gy")),
        P(None, ("gx", "gy")),
    )
    return jax.shard_map(
        per_device,
        mesh=mesh,
        in_specs=placed,
        out_specs=(P(None, "gx", "gy", None), P(None, ("gx", "gy"))),
        check_vma=False,
    )
```

profile of v0, /device:TPU:1, one launch (start us, length us, event | category | flops | bytes accessed | tf_op | source)
XLA Modules:
  0.0 91.8 jit_solution(14511970181857710152)
XLA Ops:
  0.7 0.8 fusion.51
  1.6 0.1 copy.65
  1.7 2.6 %gather_fusion.1 = f32[1536,3]{1,0:T(8,128)S(1)} fusion(f32[3,512]{0,1:T(8,128)S(1)} %copy.65, s32[2048]{0:T(1024)S(1)} %get-tuple-element.121), kind=kCustom, calls=%fused_computation.1 | custom fusion | bytes 43008 | tf_op jit(solution)/shard_map/gather | solution.py:98
  4.3 0.3 copy.68
  4.6 2.6 %gather_fusion = f32[1536,3]{1,0:T(8,128)S(1)} fusion(f32[3,512]{0,1:T(8,128)S(1)} %copy.65, s32[2048]{0:T(1024)S(1)} %get-tuple-element.122), kind=kCustom, calls=%fused_computation | custom fusion | bytes 43008 | tf_op jit(solution)/shard_map/gather | solution.py:98
  7.2 0.3 copy.67
  7.5 0.5 copy-done.2
  8.0 0.3 copy.69
  8.3 0.3 copy.70
  8.6 8.8 %scatter_custom_fusion = f32[3,512]{0,1:T(8,128)S(1)} fusion(s32[1536]{0:T(1024)S(1)} %get-tuple-element.57, f32[1536,3]{1,0:T(8,128)S(1)} %copy.69, f32[]{:T(128)} %constant.182.clone.1), kind=kCustom, calls=%fused_computation.41 | custom fusion | flops 4608 | bytes 6148 | tf_op jit(solution)/shard_map/scatter-add | solution.py:102
  17.4 8.9 %scatter_fusion = f32[3,512]{0,1:T(8,128)S(1)} fusion(f32[3,512]{0,1:T(8,128)S(1)} %scatter_custom_fusion, s32[1536]{0:T(1024)S(1)} %get-tuple-element.56, f32[1536,3]{1,0:T(8,128)S(1)} %copy.70), kind=kCustom, calls=%fused_computation.3 | custom fusion | flops 4608 | bytes 61440 | tf_op jit(solution)/shard_map/scatter-add | solution.py:104
  26.3 0.1 copy.71
  26.5 0.1 select_add_fusion
  26.6 1.0 %convolution_bitcast_fusion.1 = f32[3,160,128]{2,1,0:T(8,128)S(1)} fusion(f32[128,512]{1,0:T(8,128)S(1)} %select_add_fusion, f32[3,512]{1,0:T(4,128)S(1)} %copy.71, f32[8,512]{1,0:T(8,128)S(1)} %select_add_fusion.2, f32[20,512]{1,0:T(8,128)S(1)} %select_add_fusion.1), kind=kOutput, calls=%fused_computation.7 | convolution fusion | flops 377765888 | bytes 571392 | tf_op jit(solution)/shard_map/av,czv->caz/dot_general | solution.py:116
  27.6 0.2 copy.72
  27.8 4.4 %collective-permute-start = (f32[3,2,8,128]{3,0,2,1:T(4,128)S(1)}, f32[3,2,8,128]{3,0,2,1:T(4,128)S(1)}, u32[]{:S(2)}, u32[]{:S(2)}) collective-permute-start(f32[3,2,8,128]{3,0,2,1:T(4,128)S(1)} %get-tuple-element.79), channel_id=1, source_target_pairs={{0,64},{64,128},{128,192},{192,256},{256,320},{320,384},{384,448},... | collective-permute-start | bytes 73736 | tf_op jit(solution)/shard_map/ppermute | solution.py:38
  32.2 9.8 %collective-permute-start.1 = (f32[3,2,8,128]{3,0,2,1:T(4,128)S(1)}, f32[3,2,8,128]{3,0,2,1:T(4,128)S(1)}, u32[]{:S(2)}, u32[]{:S(2)}) collective-permute-start(f32[3,2,8,128]{3,0,2,1:T(4,128)S(1)} %get-tuple-element.78), channel_id=1, source_target_pairs={{64,0},{128,64},{192,128},{256,192},{320,256},{384,320},{448,384},... | collective-permute-start | bytes 73736 | tf_op jit(solution)/shard_map/ppermute | solution.py:39
  42.1 0.6 collective-permute-done
  42.7 0.2 collective-permute-done.1
  42.9 1.9 %collective-permute-start.2 = (f32[3,16,2,128]{3,0,2,1:T(4,128)S(1)}, f32[3,16,2,128]{3,0,2,1:T(4,128)S(1)}, u32[]{:S(2)}, u32[]{:S(2)}) collective-permute-start(f32[3,16,2,128]{3,0,2,1:T(4,128)S(1)} %get-tuple-element.81), channel_id=1, source_target_pairs={{0,1},{1,2},{2,3},{3,4},{4,5},{5,6},{6,7},{7,8},{8,9},{9,10},{10,1... | collective-permute-start | bytes 147464 | tf_op jit(solution)/shard_map/ppermute | solution.py:38
  44.9 0.1 reduce_sum.36
  45.0 6.7 %collective-permute-start.3 = (f32[3,16,2,128]{3,0,2,1:T(4,128)S(1)}, f32[3,16,2,128]{3,0,2,1:T(4,128)S(1)}, u32[]{:S(2)}, u32[]{:S(2)}) collective-permute-start(f32[3,16,2,128]{3,0,2,1:T(4,128)S(1)} %get-tuple-element.80), channel_id=1, source_target_pairs={{1,0},{2,1},{3,2},{4,3},{5,4},{6,5},{7,6},{8,7},{9,8},{10,9},{11,1... | collective-permute-start | bytes 147464 | tf_op jit(solution)/shard_map/ppermute | solution.py:39
  51.8 1.3 %collective-permute-done.3 = f32[3,16,2,128]{3,0,2,1:T(4,128)S(1)} collective-permute-done((f32[3,16,2,128]{3,0,2,1:T(4,128)S(1)}, f32[3,16,2,128]{3,0,2,1:T(4,128)S(1)}, u32[]{:S(2)}, u32[]{:S(2)}) %collective-permute-start.3) | collective-permute-done | bytes 49184 | tf_op jit(solution)/shard_map/ppermute | solution.py:39
  53.1 1.0 %multiply_reduce_fusion.1 = (f32[16,4,128]{2,1,0:T(4,128)S(1)}, f32[16,4,128]{2,1,0:T(4,128)S(1)}, f32[3,16,4,128]{3,0,2,1:T(4,128)S(1)}) fusion(f32[3,16,4,128]{3,0,2,1:T(4,128)S(1)} %fusion.21, f32[16,4,128]{2,1,0:T(4,128)S(1)} %reduce_sum.36, f32[19,3,1,1]{0,1,3,2:T(4,128)S(1)} %copy-done.3, f32[19,16,4,128]{3,2,1,0:T(4,128)S(1)} %copy-done), kind=kOutput, calls=%fused_computation.39 | convolution fusion | flops 5758976 | bytes 917732 | tf_op jit(solution)/shard_map/dot_general | solution.py:68
  54.1 0.9 fusion.66
  55.0 0.9 fusion.67
  55.9 5.3 %collective-permute-start.9 = (f32[3,2,4,128]{3,0,2,1:T(4,128)S(1)}, f32[3,2,4,128]{3,0,2,1:T(4,128)S(1)}, u32[]{:S(2)}, u32[]{:S(2)}) collective-permute-start(f32[3,2,4,128]{3,0,2,1:T(4,128)S(1)} %get-tuple-element.85), channel_id=1, source_target_pairs={{64,0},{128,64},{192,128},{256,192},{320,256},{384,320},{448,384},... | collective-permute-start | bytes 36872 | tf_op jit(solution)/shard_map/ppermute | solution.py:39
  61.3 0.9 fusion.11
  62.2 2.9 %collective-permute-start.5 = (f32[19,1,4,128]{3,1,2,0:T(1,128)S(1)}, f32[19,1,4,128]{3,1,2,0:T(1,128)S(1)}, u32[]{:S(2)}, u32[]{:S(2)}) collective-permute-start(f32[19,1,4,128]{3,1,2,0:T(1,128)S(1)} %get-tuple-element.76), channel_id=1, source_target_pairs={{64,0},{128,64},{192,128},{256,192},{320,256},{384,320},{448,384},... | collective-permute-start | bytes 116744 | tf_op jit(solution)/shard_map/ppermute | solution.py:39
  65.3 1.9 %collective-permute-start.10 = (f32[3,20,2,128]{3,0,2,1:T(4,128)S(1)}, f32[3,20,2,128]{3,0,2,1:T(4,128)S(1)}, u32[]{:S(2)}, u32[]{:S(2)}) collective-permute-start(f32[3,20,2,128]{3,0,2,1:T(4,128)S(1)} %get-tuple-element.82), channel_id=1, source_target_pairs={{0,1},{1,2},{2,3},{3,4},{4,5},{5,6},{6,7},{7,8},{8,9},{9,10},{10,1... | collective-permute-start | bytes 184328 | tf_op jit(solution)/shard_map/ppermute | solution.py:38
  67.2 7.3 %collective-permute-start.11 = (f32[3,20,2,128]{3,0,2,1:T(4,128)S(1)}, f32[3,20,2,128]{3,0,2,1:T(4,128)S(1)}, u32[]{:S(2)}, u32[]{:S(2)}) collective-permute-start(f32[3,20,2,128]{3,0,2,1:T(4,128)S(1)} %get-tuple-element.83), channel_id=1, source_target_pairs={{1,0},{2,1},{3,2},{4,3},{5,4},{6,5},{7,6},{8,7},{9,8},{10,9},{11,1... | collective-permute-start | bytes 184328 | tf_op jit(solution)/shard_map/ppermute | solution.py:39
  74.6 3.4 %collective-permute-start.7 = (f32[19,18,1,128]{3,1,2,0:T(8,128)S(1)}, f32[19,18,1,128]{3,1,2,0:T(8,128)S(1)}, u32[]{:S(2)}, u32[]{:S(2)}) collective-permute-start(f32[19,18,1,128]{3,1,2,0:T(8,128)S(1)} %get-tuple-element.67), channel_id=1, source_target_pairs={{1,0},{2,1},{3,2},{4,3},{5,4},{6,5},{7,6},{8,7},{9,8},{10,9},{11,1... | collective-permute-start | bytes 525320 | tf_op jit(solution)/shard_map/ppermute | solution.py:39
  78.0 1.9 %collective-permute-start.6 = (f32[19,18,1,128]{3,1,2,0:T(8,128)S(1)}, f32[19,18,1,128]{3,1,2,0:T(8,128)S(1)}, u32[]{:S(2)}, u32[]{:S(2)}) collective-permute-start(f32[19,18,1,128]{3,1,2,0:T(8,128)S(1)} %get-tuple-element.68), channel_id=1, source_target_pairs={{0,1},{1,2},{2,3},{3,4},{4,5},{5,6},{6,7},{7,8},{8,9},{9,10},{10,1... | collective-permute-start | bytes 525320 | tf_op jit(solution)/shard_map/ppermute | solution.py:38
  80.0 0.1 pad_maximum_fusion
  80.1 1.5 %fusion.1 = f32[3,512]{1,0:T(4,128)} fusion(f32[128,512]{1,0:T(8,128)S(1)} %select_add_fusion, f32[3,20,8,128]{3,0,2,1:T(4,128)S(1)} %pad_maximum_fusion, f32[8,512]{1,0:T(8,128)S(1)} %select_add_fusion.2, f32[20,512]{1,0:T(8,128)S(1)} %select_add_fusion.1), kind=kOutput, calls=%fused_computation.6 | convolution fusion | flops 377960960 | bytes 571392 | tf_op jit(solution)/shard_map/av,caz->czv/dot_general | solution.py:146
  81.6 7.5 %collective-permute-done.6 = f32[19,18,1,128]{3,1,2,0:T(8,128)S(1)} collective-permute-done((f32[19,18,1,128]{3,1,2,0:T(8,128)S(1)}, f32[19,18,1,128]{3,1,2,0:T(8,128)S(1)}, u32[]{:S(2)}, u32[]{:S(2)}) %collective-permute-start.6) | collective-permute-done | bytes 175136 | tf_op jit(solution)/shard_map/ppermute | solution.py:38
  89.2 0.1 constant_dynamic-update-slice_fusion.13
  89.3 0.1 constant_dynamic-update-slice_fusion.12
  89.7 0.1 slice.512
  90.1 0.1 constant_dynamic-update-slice_fusion.7
  90.2 0.1 constant_dynamic-update-slice_fusion.6
  90.3 0.1 constant_dynamic-update-slice_fusion.5
  90.3 0.1 constant_dynamic-update-slice_fusion.4
  90.4 0.1 constant_dynamic-update-slice_fusion.3
  90.5 0.1 constant_dynamic-update-slice_fusion.2
  90.6 0.1 constant_dynamic-update-slice_fusion.1
  90.7 0.1 constant_dynamic-update-slice_fusion
  90.8 1.1 %copy.84 = f32[19,16,4,128]{3,2,1,0:T(4,128)} copy(f32[19,16,4,128]{3,1,2,0:T(8,128)S(1)} %constant_dynamic-update-slice_fusion) | data formatting | bytes 1245184
  (68 shorter events, 1.5 us)
Async XLA Ops:
  0.6 0.9 copy-start.1
  0.6 0.9 copy-start.4
  7.2 0.7 copy-start.2
  7.2 0.7 copy-start.5
  27.8 17.1 %copy-start = (f32[19,16,4,128]{3,2,1,0:T(4,128)S(1)}, f32[19,16,4,128]{3,2,1,0:T(4,128)}, u32[]{:S(2)}) copy-start(f32[19,16,4,128]{3,2,1,0:T(4,128)} %param.16) | copy-start | bytes 1867780
  27.8 14.9 %collective-permute-start = (f32[3,2,8,128]{3,0,2,1:T(4,128)S(1)}, f32[3,2,8,128]{3,0,2,1:T(4,128)S(1)}, u32[]{:S(2)}, u32[]{:S(2)}) collective-permute-start(f32[3,2,8,128]{3,0,2,1:T(4,128)S(1)} %get-tuple-element.79), channel_id=1, source_target_pairs={{0,64},{64,128},{128,192},{192,256},{256,320},{320,384},{384,448},... | collective-permute-start | bytes 73736 | tf_op jit(solution)/shard_map/ppermute | solution.py:38
  32.2 10.7 %collective-permute-start.1 = (f32[3,2,8,128]{3,0,2,1:T(4,128)S(1)}, f32[3,2,8,128]{3,0,2,1:T(4,128)S(1)}, u32[]{:S(2)}, u32[]{:S(2)}) collective-permute-start(f32[3,2,8,128]{3,0,2,1:T(4,128)S(1)} %get-tuple-element.78), channel_id=1, source_target_pairs={{64,0},{128,64},{192,128},{256,192},{320,256},{384,320},{448,384},... | collective-permute-start | bytes 73736 | tf_op jit(solution)/shard_map/ppermute | solution.py:39
  42.9 8.8 %collective-permute-start.2 = (f32[3,16,2,128]{3,0,2,1:T(4,128)S(1)}, f32[3,16,2,128]{3,0,2,1:T(4,128)S(1)}, u32[]{:S(2)}, u32[]{:S(2)}) collective-permute-start(f32[3,16,2,128]{3,0,2,1:T(4,128)S(1)} %get-tuple-element.81), channel_id=1, source_target_pairs={{0,1},{1,2},{2,3},{3,4},{4,5},{5,6},{6,7},{7,8},{8,9},{9,10},{10,1... | collective-permute-start | bytes 147464 | tf_op jit(solution)/shard_map/ppermute | solution.py:38
  45.0 8.0 %collective-permute-start.3 = (f32[3,16,2,128]{3,0,2,1:T(4,128)S(1)}, f32[3,16,2,128]{3,0,2,1:T(4,128)S(1)}, u32[]{:S(2)}, u32[]{:S(2)}) collective-permute-start(f32[3,16,2,128]{3,0,2,1:T(4,128)S(1)} %get-tuple-element.80), channel_id=1, source_target_pairs={{1,0},{2,1},{3,2},{4,3},{5,4},{6,5},{7,6},{8,7},{9,8},{10,9},{11,1... | collective-permute-start | bytes 147464 | tf_op jit(solution)/shard_map/ppermute | solution.py:39
  51.7 1.3 %copy-start.3 = (f32[19,3,1,1]{0,1,3,2:T(4,128)S(1)}, f32[19,3,1,1]{0,1,3,2:T(4,128)}, u32[]{:S(2)}) copy-start(f32[19,3,1,1]{0,1,3,2:T(4,128)} %constant.220) | copy-start | bytes 688
  55.9 5.4 %copy-start.6 = (f32[19]{0:T(128)S(1)}, f32[19]{0:T(128)}, u32[]{:S(2)}) copy-start(f32[19]{0:T(128)} %constant.219) | copy-start | bytes 232
  55.9 5.4 %copy-start.7 = (f32[19]{0:T(128)S(1)}, f32[19]{0:T(128)}, u32[]{:S(2)}) copy-start(f32[19]{0:T(128)} %constant.212.clone) | copy-start | bytes 232
  55.9 9.3 %collective-permute-start.8 = (f32[3,2,4,128]{3,0,2,1:T(4,128)S(1)}, f32[3,2,4,128]{3,0,2,1:T(4,128)S(1)}, u32[]{:S(2)}, u32[]{:S(2)}) collective-permute-start(f32[3,2,4,128]{3,0,2,1:T(4,128)S(1)} %get-tuple-element.84), channel_id=1, source_target_pairs={{0,64},{64,128},{128,192},{192,256},{256,320},{320,384},{384,448},... | collective-permute-start | bytes 36872 | tf_op jit(solution)/shard_map/ppermute | solution.py:38
  55.9 9.2 %collective-permute-start.9 = (f32[3,2,4,128]{3,0,2,1:T(4,128)S(1)}, f32[3,2,4,128]{3,0,2,1:T(4,128)S(1)}, u32[]{:S(2)}, u32[]{:S(2)}) collective-permute-start(f32[3,2,4,128]{3,0,2,1:T(4,128)S(1)} %get-tuple-element.85), channel_id=1, source_target_pairs={{64,0},{128,64},{192,128},{256,192},{320,256},{384,320},{448,384},... | collective-permute-start | bytes 36872 | tf_op jit(solution)/shard_map/ppermute | solution.py:39
  62.2 12.3 %collective-permute-start.5 = (f32[19,1,4,128]{3,1,2,0:T(1,128)S(1)}, f32[19,1,4,128]{3,1,2,0:T(1,128)S(1)}, u32[]{:S(2)}, u32[]{:S(2)}) collective-permute-start(f32[19,1,4,128]{3,1,2,0:T(1,128)S(1)} %get-tuple-element.76), channel_id=1, source_target_pairs={{64,0},{128,64},{192,128},{256,192},{320,256},{384,320},{448,384},... | collective-permute-start | bytes 116744 | tf_op jit(solution)/shard_map/ppermute | solution.py:39
  65.2 9.4 %collective-permute-start.4 = (f32[19,1,4,128]{3,1,2,0:T(1,128)S(1)}, f32[19,1,4,128]{3,1,2,0:T(1,128)S(1)}, u32[]{:S(2)}, u32[]{:S(2)}) collective-permute-start(f32[19,1,4,128]{3,1,2,0:T(1,128)S(1)} %get-tuple-element.77), channel_id=1, source_target_pairs={{0,64},{64,128},{128,192},{192,256},{256,320},{320,384},{384,448},... | collective-permute-start | bytes 116744 | tf_op jit(solution)/shard_map/ppermute | solution.py:38
  65.3 14.7 %collective-permute-start.10 = (f32[3,20,2,128]{3,0,2,1:T(4,128)S(1)}, f32[3,20,2,128]{3,0,2,1:T(4,128)S(1)}, u32[]{:S(2)}, u32[]{:S(2)}) collective-permute-start(f32[3,20,2,128]{3,0,2,1:T(4,128)S(1)} %get-tuple-element.82), channel_id=1, source_target_pairs={{0,1},{1,2},{2,3},{3,4},{4,5},{5,6},{6,7},{7,8},{8,9},{9,10},{10,1... | collective-permute-start | bytes 184328 | tf_op jit(solution)/shard_map/ppermute | solution.py:38
  67.2 12.8 %collective-permute-start.11 = (f32[3,20,2,128]{3,0,2,1:T(4,128)S(1)}, f32[3,20,2,128]{3,0,2,1:T(4,128)S(1)}, u32[]{:S(2)}, u32[]{:S(2)}) collective-permute-start(f32[3,20,2,128]{3,0,2,1:T(4,128)S(1)} %get-tuple-element.83), channel_id=1, source_target_pairs={{1,0},{2,1},{3,2},{4,3},{5,4},{6,5},{7,6},{8,7},{9,8},{10,9},{11,1... | collective-permute-start | bytes 184328 | tf_op jit(solution)/shard_map/ppermute | solution.py:39
  74.6 14.4 %collective-permute-start.7 = (f32[19,18,1,128]{3,1,2,0:T(8,128)S(1)}, f32[19,18,1,128]{3,1,2,0:T(8,128)S(1)}, u32[]{:S(2)}, u32[]{:S(2)}) collective-permute-start(f32[19,18,1,128]{3,1,2,0:T(8,128)S(1)} %get-tuple-element.67), channel_id=1, source_target_pairs={{1,0},{2,1},{3,2},{4,3},{5,4},{6,5},{7,6},{8,7},{9,8},{10,9},{11,1... | collective-permute-start | bytes 525320 | tf_op jit(solution)/shard_map/ppermute | solution.py:39
  78.0 11.1 %collective-permute-start.6 = (f32[19,18,1,128]{3,1,2,0:T(8,128)S(1)}, f32[19,18,1,128]{3,1,2,0:T(8,128)S(1)}, u32[]{:S(2)}, u32[]{:S(2)}) collective-permute-start(f32[19,18,1,128]{3,1,2,0:T(8,128)S(1)} %get-tuple-element.68), channel_id=1, source_target_pairs={{0,1},{1,2},{2,3},{3,4},{4,5},{5,6},{6,7},{7,8},{8,9},{9,10},{10,1... | collective-permute-start | bytes 525320 | tf_op jit(solution)/shard_map/ppermute | solution.py:38
where the time goes:
time: 92.2 us; the launch traced here: 91.8 us
  starting transfers between devices  45.6 us (49%)
  other arithmetic  21 us (23%)
  waiting for transfers between devices  9.52 us (10%)
  local copies, waits for them, and re-layouts  9.31 us (10%)
  matrix products  5.26 us (6%)
  between operations  1.17 us (1%)
    ppermute x6, starting transfers between devices, with_halo(): after = lax.ppermute(initial, axis, down)  35.4 us
    scatter-add x2, other arithmetic, per_device(): membrane = jnp.zeros((3, count), jnp.float32).at[:, edges[0]].add(stretch...  17.7 us
    ppermute x6, starting transfers between devices, with_halo(): before = lax.ppermute(last, axis, up)  10.2 us
    ppermute x6, waiting for transfers between devices, with_halo(): before = lax.ppermute(last, axis, up)  8.09 us
    gather x2, local copies, waits for them, and re-layouts, per_device(): position[:, edges[1]] - position[:, edges[0]] - rest  2.86 us
    gather x2, local copies, waits for them, and re-layouts, per_device(): position[:, edges[0]]  2.86 us
  transfers between devices with their start and end apart: 12, of which 4 were waited for; matrix products, arithmetic and copies ran while one was open for 3% of the time, Pallas kernels for 0%

commit v1 on v0

v1 whole, which is shorter than its diff:
```python
import jax
import jax.numpy as jnp
from jax import lax
from jax.experimental import pallas as pl
from jax.experimental.pallas import tpu as pltpu
from jax.sharding import PartitionSpec as P

lattice_speeds = [
    (0, 0, 0),
    (1, 0, 0),
    (-1, 0, 0),
    (0, 1, 0),
    (0, -1, 0),
    (0, 0, 1),
    (0, 0, -1),
    (1, 1, 0),
    (-1, -1, 0),
    (1, -1, 0),
    (-1, 1, 0),
    (1, 0, 1),
    (-1, 0, -1),
    (1, 0, -1),
    (-1, 0, 1),
    (0, 1, 1),
    (0, -1, -1),
    (0, 1, -1),
    (0, -1, 1),
]
lattice_weights = [1.0 / 3.0] + [1.0 / 18.0] * 6 + [1.0 / 36.0] * 12
relax_time = 0.9

f32 = jnp.float32
bf16 = jnp.bfloat16

WX, WY, NZ = 16, 4, 128
CELLS = WX * WY
VERTS, TILE, EDGES = 512, 128, 1536
SX, SY = 24, 7

UP_Y = [q for q in range(19) if lattice_speeds[q][1] == 1]
DOWN_Y = [q for q in range(19) if lattice_speeds[q][1] == -1]
UP_X = [q for q in range(19) if lattice_speeds[q][0] == 1]
DOWN_X = [q for q in range(19) if lattice_speeds[q][0] == -1]

FORCE_ROWS = 9 * WX + 3 * 16
UP_ROWS = FORCE_ROWS + 4 * WX + 5 * WX
DOWN_ROWS = FORCE_ROWS + 8 * WX + 5 * WX
RIGHT_ROWS = 3 * 24 + 32 + 24
LEFT_ROWS = 3 * 24 + 2 * 32 + 24


def outer_weight(r):
    return (5.0 - 2.0 * r - jnp.sqrt(-7.0 + 12.0 * r - 4.0 * r * r)) / 8.0


def inner_weight(r):
    return (3.0 - 2.0 * r + jnp.sqrt(1.0 + 4.0 * r - 4.0 * r * r)) / 8.0


def halves(value):
    high = value.astype(bf16)
    low = (value - high.astype(f32)).astype(bf16)
    return high, low


def along_last(a, b):
    return lax.dot_general(a, b, (((1,), (1,)), ((), ())), preferred_element_type=f32)


def iota(shape, dim):
    return lax.broadcasted_iota(jnp.int32, shape, dim)


def edge_forces(base, frac, edges, stiffness, rest):
    head = edges[0:1]
    tail = edges[1:2]
    run = head >> 7
    local = iota((TILE, EDGES), 0)
    plus = local == (tail & (TILE - 1))
    minus = local == (head & (TILE - 1))
    signed = jnp.where(plus, 1.0, jnp.where(minus, -1.0, 0.0)).astype(bf16)
    whole = base.astype(f32)
    high, low = halves(frac)
    blank = jnp.zeros((5, TILE), f32)
    pieces = []
    for part in (whole, high.astype(f32), low.astype(f32)):
        for t in range(4):
            pieces += [part[:, t * TILE : (t + 1) * TILE], blank]
    stacked = jnp.concatenate(pieces, axis=0).astype(bf16)
    found = jnp.dot(stacked, signed, preferred_element_type=f32)
    found = found[0:32] + found[32:64] + found[64:96]
    apart = jnp.zeros((8, EDGES), f32)
    for t in range(4):
        apart = apart + jnp.where(run == t, found[8 * t : 8 * t + 8], 0.0)
    stretch = stiffness * (apart[0:3] - rest)
    high, low = halves(stretch)
    blank = jnp.zeros((5, EDGES), f32)
    pieces = []
    for part in (high.astype(f32), low.astype(f32)):
        for t in range(4):
            pieces += [jnp.where(run == t, part, 0.0), blank]
    stacked = jnp.concatenate(pieces, axis=0).astype(bf16)
    pulled = along_last(stacked, signed)
    pulled = pulled[0:32] + pulled[32:64]
    return jnp.concatenate([-pulled[8 * t : 8 * t + 3] for t in range(4)], axis=1)


def spread_kernel(
    pop, base, frac, edges, stiffness, rest, force, moment, plane_out, high_out, low_out, edge_out, up, down
):
    membrane = edge_forces(base[...], frac[...], edges[...], stiffness[...], rest[...])
    part = frac[...]
    kernel = [
        outer_weight(1.0 + part),
        inner_weight(part),
        inner_weight(1.0 - part),
        outer_weight(2.0 - part),
    ]
    cell = base[...]

    def columns(rows, offset, dim):
        total = jnp.zeros((rows, VERTS), f32)
        for step in range(4):
            total = jnp.where(offset == step, kernel[step][dim : dim + 1], total)
        return total

    slot = iota((SX, VERTS), 0)
    slot = jnp.where(slot == SX - 1, -1, slot)
    along_x = columns(SX, slot - (cell[0:1] & (WX - 1)) + 1, 0)
    slab = iota((8, VERTS), 0)
    along_y = columns(8, slab - (cell[1:2] & (WY - 1)), 1)
    depth = iota((NZ, VERTS), 0)
    along_z = columns(NZ, (depth - cell[2:3] + 1) & (NZ - 1), 2)
    plane = jnp.concatenate([along_x * along_y[y : y + 1] for y in range(SY)], axis=0)
    plane_out[...] = plane
    z_high, z_low = halves(along_z)
    high_out[...] = z_high
    low_out[...] = z_low

    density = pop[0:CELLS]
    moments = [None, None, None]
    for q in range(1, 19):
        value = pop[q * CELLS : (q + 1) * CELLS]
        density = density + value
        for d in range(3):
            c = lattice_speeds[q][d]
            if c:
                if moments[d] is None:
                    moments[d] = value if c > 0 else -value
                else:
                    moments[d] = moments[d] + value if c > 0 else moments[d] - value
    moment[0:CELLS] = density
    for d in range(3):
        moment[(d + 1) * CELLS : (d + 2) * CELLS] = moments[d]

    plane_high, plane_low = halves(plane)
    for c in range(3):
        load_high, load_low = halves(along_z * membrane[c : c + 1])
        result = (
            along_last(plane_high, load_high)
            + along_last(plane_low, load_high)
            + along_last(plane_high, load_low)
        )
        for y in range(SY):
            force[(y * 3 + c) * SX : (y * 3 + c + 1) * SX] = result[y * SX : (y + 1) * SX]

    def strips(out, slab, rows, dirs, edge_row):
        at = 0
        for k in range(9):
            out[at : at + WX] = force[(slab * 3 + k) * SX : (slab * 3 + k) * SX + WX]
            at += WX
        for x in (16, 17, 23):
            out[at : at + 9] = force[pl.ds(slab * 3 * SX + x, 9, stride=SX), :]
            at += 16
        for y in rows:
            for q in range(4):
                out[at : at + WX] = moment[pl.ds(q * CELLS + y, WX, stride=WY), :]
                at += WX
        for q in dirs:
            out[at : at + WX] = pop[pl.ds(q * CELLS + edge_row, WX, stride=WY), :]
            at += WX

    strips(up, 4, (3,), UP_Y, 3)
    strips(down, 0, (0, 1), DOWN_Y, 0)
    for k, q in enumerate(UP_X):
        edge_out[k * 4 : k * 4 + 4] = pop[q * CELLS + 60 : q * CELLS + 64]
    for k, q in enumerate(DOWN_X):
        edge_out[24 + k * 4 : 24 + k * 4 + 4] = pop[q * CELLS : q * CELLS + 4]


def merge_kernel(force_in, moment, edge, below, above, force, right, left):
    def outer(block, slab):
        for k in range(9):
            row = (slab * 3 + k) * SX
            force[row : row + WX] = force_in[row : row + WX] + block[k * WX : k * WX + WX]
        for n, x in enumerate((16, 17, 23)):
            rows = pl.ds(slab * 3 * SX + x, 9, stride=SX)
            at = 9 * WX + 16 * n
            force[rows, :] = force_in[rows, :] + block[at : at + 9]

    for k in range(9, 12):
        force[k * SX : (k + 1) * SX] = force_in[k * SX : (k + 1) * SX]
    for slab in (0, 4):
        for k in range(9):
            row = (slab * 3 + k) * SX + 16
            force[row : row + 8] = force_in[row : row + 8]
    outer(below, 0)
    outer(above, 4)

    def outgoing(out, sources, columns, offset, dirs):
        at = 0
        for x in sources:
            out[at : at + 21] = force[pl.ds(x, 21, stride=SX), :]
            at += 24
        for x in columns:
            out[at : at + 4] = below[pl.ds(FORCE_ROWS + x, 4, stride=WX), :]
            for y in range(4):
                out[at + 4 + y * 4 : at + 8 + y * 4] = moment[pl.ds(x * 4 + y, 4, stride=CELLS), :]
            out[at + 20 : at + 24] = above[pl.ds(FORCE_ROWS + x, 4, stride=WX), :]
            out[at + 24 : at + 28] = above[pl.ds(FORCE_ROWS + 4 * WX + x, 4, stride=WX), :]
            at += 32
        x = columns[0]
        for k, q in enumerate(dirs):
            row = offset + k * 4
            step = lattice_speeds[q][1]
            if step == 0:
                out[at : at + 4] = edge[row : row + 4]
            elif step == 1:
                source = FORCE_ROWS + 4 * WX + UP_Y.index(q) * WX + x
                out[at : at + 1] = below[source : source + 1]
                out[at + 1 : at + 4] = edge[row : row + 3]
            else:
                source = FORCE_ROWS + 8 * WX + DOWN_Y.index(q) * WX + x
                out[at : at + 3] = edge[row + 1 : row + 4]
                out[at + 3 : at + 4] = above[source : source + 1]
            at += 4

    outgoing(right, (15, 16, 17), (15,), 0, UP_X)
    outgoing(left, (23, 0, 1), (0, 1), 24, DOWN_X)


def collide_kernel(
    pop, force_in, moment, below, above, west, east, plane, z_high, z_low, fresh, sampled, force, ext, speed
):
    force[...] = force_in[...]
    for n, x in enumerate((23, 0, 1)):
        rows = pl.ds(x, 21, stride=SX)
        force[rows, :] = force[rows, :] + west[24 * n : 24 * n + 21]
    for n, x in enumerate((15, 16, 17)):
        rows = pl.ds(x, 21, stride=SX)
        force[rows, :] = force[rows, :] + east[24 * n : 24 * n + 21]

    for slab in range(SY):
        for q in range(4):
            row = (slab * 4 + q) * SX
            if slab == 0:
                value = below[FORCE_ROWS + q * WX : FORCE_ROWS + (q + 1) * WX]
            elif slab < 5:
                value = moment[pl.ds(q * CELLS + slab - 1, WX, stride=WY), :]
            else:
                source = FORCE_ROWS + ((slab - 5) * 4 + q) * WX
                value = above[source : source + WX]
            ext[row : row + WX] = value
            ext[row + WX : row + SX] = jnp.ones((8, NZ), f32)
    ext[pl.ds(23, 28, stride=SX), :] = west[72 : 72 + 28]
    ext[pl.ds(16, 28, stride=SX), :] = east[72 : 72 + 28]
    ext[pl.ds(17, 28, stride=SX), :] = east[104 : 104 + 28]

    rate = 1.0 / relax_time
    gain = 1.0 - 0.5 / relax_time
    for slab in range(SY):
        density = ext[slab * 4 * SX : (slab * 4 + 1) * SX]
        inverse = 1.0 / density
        pull = [force[(slab * 3 + c) * SX : (slab * 3 + c + 1) * SX] for c in range(3)]
        flow = [
            (ext[(slab * 4 + 1 + c) * SX : (slab * 4 + 2 + c) * SX] + 0.5 * pull[c]) * inverse
            for c in range(3)
        ]
        for c in range(3):
            high, low = halves(flow[c])
            row = (c * SY + slab) * SX
            speed[row : row + SX, 0:NZ] = high.astype(f32)
            speed[row : row + SX, NZ : 2 * NZ] = low.astype(f32)
        if slab == SY - 1:
            continue
        y_from = slab - 1
        square = flow[0] * flow[0] + flow[1] * flow[1] + flow[2] * flow[2]
        work = flow[0] * pull[0] + flow[1] * pull[1] + flow[2] * pull[2]
        scaled = rate * density
        constant = scaled * (1.0 - 1.5 * square) - (3.0 * gain) * work
        linear = 3.0 * scaled
        quadratic = 4.5 * scaled
        for q in range(19):
            step_x, step_y, step_z = lattice_speeds[q]
            y_to = y_from + step_y
            if y_to < 0 or y_to > 3:
                continue
            if 0 <= y_from <= 3:
                value = pop[pl.ds(q * CELLS + y_from, WX, stride=WY), :]
            elif y_from < 0:
                source = FORCE_ROWS + 4 * WX + UP_Y.index(q) * WX
                value = below[source : source + WX]
            else:
                source = FORCE_ROWS + 8 * WX + DOWN_Y.index(q) * WX
                value = above[source : source + WX]
            if step_x == 1:
                row = 104 + UP_X.index(q) * 4 + y_to
                value = jnp.concatenate(
                    [value, jnp.broadcast_to(west[row : row + 1], (8, NZ))], axis=0
                )
            elif step_x == -1:
                row = 136 + DOWN_X.index(q) * 4 + y_to
                value = jnp.concatenate(
                    [value, jnp.broadcast_to(east[row : row + 1], (8, NZ))], axis=0
                )
            extent = value.shape[0]

            def directed(vectors):
                total = None
                for c in range(3):
                    s = lattice_speeds[q][c]
                    if s:
                        term = vectors[c][0:extent]
                        if total is None:
                            total = term if s > 0 else -term
                        else:
                            total = total + term if s > 0 else total - term
                return total

            balance = constant[0:extent]
            if q:
                cu = directed(flow)
                cf = directed(pull)
                balance = (
                    balance
                    + cu * (linear[0:extent] + quadratic[0:extent] * cu + (9.0 * gain) * cf)
                    + (3.0 * gain) * cf
                )
            post = (1.0 - rate) * value + lattice_weights[q] * balance
            if step_x:
                post = pltpu.roll(post, step_x % SX, 0)[0:WX]
            if step_z:
                post = pltpu.roll(post, step_z % NZ, 1)
            fresh[pl.ds(q * CELLS + y_to, WX, stride=WY), :] = post

    both = jnp.concatenate([z_high[...], z_high[...]], axis=0)
    rows = SY * SX
    for c in range(3):
        split = speed[c * rows : (c + 1) * rows].astype(bf16)
        value = jnp.dot(split, both, preferred_element_type=f32) + jnp.dot(
            split[:, 0:NZ], z_low[...], preferred_element_type=f32
        )
        sampled[c : c + 1] = jnp.sum(value * plane[...], axis=0, keepdims=True)


def call(kernel, outputs, scratch, name, operands):
    vmem = pl.BlockSpec(memory_space=pltpu.VMEM)
    return pl.pallas_call(
        kernel,
        out_shape=[jax.ShapeDtypeStruct(shape, kind) for shape, kind in outputs],
        in_specs=[vmem] * len(operands),
        out_specs=[vmem] * len(outputs),
        scratch_shapes=[pltpu.VMEM(shape, f32) for shape in scratch],
        compiler_params=pltpu.CompilerParams(vmem_limit_bytes=32 * 1024 * 1024),
        name=name,
    )(*operands)


def shift(value, axis, step):
    size = lax.axis_size(axis)
    return lax.ppermute(value, axis, [(i, (i + step) % size) for i in range(size)])


def per_device(populations, vert_base, vert_frac, edges, stiffness, rest):
    pop = populations.reshape(19 * CELLS, NZ)
    force, moment, plane, z_high, z_low, edge, up, down = call(
        spread_kernel,
        [
            ((SY * 3 * SX, NZ), f32),
            ((4 * CELLS, NZ), f32),
            ((SY * SX, VERTS), f32),
            ((NZ, VERTS), bf16),
            ((NZ, VERTS), bf16),
            ((48, NZ), f32),
            ((UP_ROWS, NZ), f32),
            ((DOWN_ROWS, NZ), f32),
        ],
        [],
        "spread",
        [pop, vert_base, vert_frac, edges, stiffness.reshape(1, EDGES), rest],
    )
    below = shift(up, "gy", 1)
    above = shift(down, "gy", -1)
    force, right, left = call(
        merge_kernel,
        [((SY * 3 * SX, NZ), f32), ((RIGHT_ROWS, NZ), f32), ((LEFT_ROWS, NZ), f32)],
        [],
        "merge",
        [force, moment, edge, below, above],
    )
    west = shift(right, "gx", 1)
    east = shift(left, "gx", -1)
    fresh, sampled = call(
        collide_kernel,
        [((19 * CELLS, NZ), f32), ((3, VERTS), f32)],
        [(SY * 3 * SX, NZ), (SY * 4 * SX, NZ), (SY * 3 * SX, 2 * NZ)],
        "collide",
        [pop, force, moment, below, above, west, east, plane, z_high, z_low],
    )
    return fresh.reshape(19, WX, WY, NZ), sampled


def solution(mesh):
    placed = (
        P(None, "gx", "gy", None),
        P(None, ("gx", "gy")),
        P(None, ("gx", "gy")),
        P(None, ("gx", "gy")),
        P(("gx", "gy")),
        P(None, ("gx", "gy")),
    )
    return jax.shard_map(
        per_device,
        mesh=mesh,
        in_specs=placed,
        out_specs=(P(None, "gx", "gy", None), P(None, ("gx", "gy"))),
        check_vma=False,
    )
```

time: 92.2 us -> 43.8 us (0.48)
  the two profiles are of different devices: /device:TPU:1 before, /device:TPU:8 now
where the time goes in v1:
time: 43.8 us; the launch traced here: 43.4 us
  starting transfers between devices  21.7 us (50%)
  waiting for transfers between devices  14 us (32%)
  local copies, waits for them, and re-layouts  3.92 us (9%)
  Pallas kernels  3.02 us (7%)
  between operations  0.67 us (2%)
    ppermute x4, starting transfers between devices, shift(): lax.ppermute(value, axis, [(i, (i + step) % size) for i in range(size)])  21.7 us
    ppermute x4, waiting for transfers between devices, shift(): lax.ppermute(value, axis, [(i, (i + step) % size) for i in range(size)])  14 us
    unnamed x12, local copies, waits for them, and re-layouts  3.21 us
    pallas_call x3, Pallas kernels, call(): pl.pallas_call(kernel, out_shape=[jax.ShapeDtypeStruct(shape, kind) for s...  3.02 us
  transfers between devices with their start and end apart: 4, of which 2 were waited for; matrix products, arithmetic and copies ran while one was open for 0% of the time, Pallas kernels for 0%

profile of v1, /device:TPU:8, one launch (start us, length us, event | category | flops | bytes accessed | tf_op | source)
XLA Modules:
  0.0 43.4 jit_solution(417721856857876046)
XLA Ops:
  0.6 0.0 copy-start.3
  0.6 0.7 %reshape.14.stiffness = f32[1,1536]{1,0:T(1,128)S(1)} reshape(f32[1536]{0:T(1024)} %param.10) | data formatting | bytes 12288 | tf_op jit(solution)/shard_map/reshape | solution.py:390
  1.3 0.0 copy-done.3
  1.4 0.0 copy-start
  1.4 1.1 %copy-done = f32[19,16,4,128]{3,2,1,0:T(4,128)S(1)} copy-done((f32[19,16,4,128]{3,2,1,0:T(4,128)S(1)}, f32[19,16,4,128]{3,2,1,0:T(4,128)}, u32[]{:S(2)}) %copy-start) | copy-done | bytes 622616
  2.4 0.0 copy-start.2
  2.4 0.7 %copy-done.2 = f32[3,1536]{1,0:T(4,128)S(1)} copy-done((f32[3,1536]{1,0:T(4,128)S(1)}, f32[3,1536]{1,0:T(4,128)}, u32[]{:S(2)}) %copy-start.2) | copy-done | bytes 18456
  3.2 0.0 copy-start.4
  3.2 0.7 %copy-done.4 = s32[3,512]{1,0:T(4,128)S(1)} copy-done((s32[3,512]{1,0:T(4,128)S(1)}, s32[3,512]{1,0:T(4,128)}, u32[]{:S(2)}) %copy-start.4) | copy-done | bytes 6168
  3.9 0.0 copy-start.5
  3.9 0.7 %copy-done.5 = f32[3,512]{1,0:T(4,128)S(1)} copy-done((f32[3,512]{1,0:T(4,128)S(1)}, f32[3,512]{1,0:T(4,128)}, u32[]{:S(2)}) %copy-start.5) | copy-done | bytes 6168
  4.6 0.0 copy-start.1
  4.6 1.3 %spread.1 = (f32[504,128]{1,0:T(8,128)S(1)}, f32[256,128]{1,0:T(8,128)S(1)}, f32[168,512]{1,0:T(8,128)S(1)}, bf16[128,512]{1,0:T(8,128)(2,1)S(1)}, bf16[128,512]...) custom-call(f32[1216,128]{1,0:T(8,128)S(1)} %bitcast.2, ...), custom_call_target="tpu_custom_call" | custom-call | tf_op jit(solution)/shard_map/spread/pallas_call | solution.py:358
  5.9 6.2 %collective-permute-start.1 = (f32[400,128]{1,0:T(8,128)S(1)}, f32[400,128]{1,0:T(8,128)S(1)}, u32[]{:S(2)}, u32[]{:S(2)}) collective-permute-start(f32[400,128]{1,0:T(8,128)S(1)} %get-tuple-element.19), channel_id=1, source_target_pairs={{0,63},{1,0},{2,1},{3,2},{4,3},{5,4},{6,5},{7,6},{8,7},{9,8},{10,9... | collective-permute-start | bytes 614408 | tf_op jit(solution)/shard_map/ppermute | solution.py:371
  12.0 1.9 %collective-permute-start = (f32[336,128]{1,0:T(8,128)S(1)}, f32[336,128]{1,0:T(8,128)S(1)}, u32[]{:S(2)}, u32[]{:S(2)}) collective-permute-start(f32[336,128]{1,0:T(8,128)S(1)} %get-tuple-element.18), channel_id=1, source_target_pairs={{0,1},{1,2},{2,3},{3,4},{4,5},{5,6},{6,7},{7,8},{8,9},{9,10},{10,1... | collective-permute-start | bytes 516104 | tf_op jit(solution)/shard_map/ppermute | solution.py:371
  13.9 9.1 %collective-permute-done.below = f32[336,128]{1,0:T(8,128)S(1)} collective-permute-done((f32[336,128]{1,0:T(8,128)S(1)}, f32[336,128]{1,0:T(8,128)S(1)}, u32[]{:S(2)}, u32[]{:S(2)}) %collective-permute-start) | collective-permute-done | bytes 172064 | tf_op jit(solution)/shard_map/ppermute | solution.py:371
  23.1 0.0 collective-permute-done.1.above
  23.1 0.1 merge.1
  23.1 13.7 %collective-permute-start.3 = (f32[160,128]{1,0:T(8,128)S(1)}, f32[160,128]{1,0:T(8,128)S(1)}, u32[]{:S(2)}, u32[]{:S(2)}) collective-permute-start(f32[160,128]{1,0:T(8,128)S(1)} %get-tuple-element.22), channel_id=1, source_target_pairs={{0,960},{64,0},{128,64},{192,128},{256,192},{320,256},{384,320},{4... | collective-permute-start | bytes 245768 | tf_op jit(solution)/shard_map/ppermute | solution.py:371
  36.8 0.0 collective-permute-start.2
  36.8 4.9 %collective-permute-done.2.west = f32[128,128]{1,0:T(8,128)S(1)} collective-permute-done((f32[128,128]{1,0:T(8,128)S(1)}, f32[128,128]{1,0:T(8,128)S(1)}, u32[]{:S(2)}, u32[]{:S(2)}) %collective-permute-start.2) | collective-permute-done | bytes 65568 | tf_op jit(solution)/shard_map/ppermute | solution.py:371
  41.7 0.0 collective-permute-done.3.east
  41.7 0.0 copy-done.1
  41.7 1.6 %collide.1 = (f32[1216,128]{1,0:T(8,128)}, f32[3,512]{1,0:T(4,128)}) custom-call(f32[1216,128]{1,0:T(8,128)S(1)} %bitcast.3, f32[504,128]{1,0:T(8,128)S(1)} %get-tuple-element.20.force_in, f32[256,128]{1,0:T(8,128)S(1)} %get-tuple-element.16.moment, f32[336,128]{1,0:T(8,128)S(1)} %collective-permute-done.below, f32[400,128]{1,0:T(8,128)S(1)} %collective-permute-done.1.above, ...), custom_call_target="tpu_custom_call" | custom-call | tf_op jit(solution)/shard_map/collide/pallas_call | solution.py:358
Async XLA Ops:
  0.6 0.7 %copy-start.3 = (s32[2,1536]{1,0:T(2,128)S(1)}, s32[2,1536]{1,0:T(2,128)}, u32[]{:S(2)}) copy-start(s32[2,1536]{1,0:T(2,128)} %edges.1) | copy-start | bytes 36868
  1.4 1.1 %copy-start = (f32[19,16,4,128]{3,2,1,0:T(4,128)S(1)}, f32[19,16,4,128]{3,2,1,0:T(4,128)}, u32[]{:S(2)}) copy-start(f32[19,16,4,128]{3,2,1,0:T(4,128)} %param.6) | copy-start | bytes 1867780
  2.4 0.7 %copy-start.2 = (f32[3,1536]{1,0:T(4,128)S(1)}, f32[3,1536]{1,0:T(4,128)}, u32[]{:S(2)}) copy-start(f32[3,1536]{1,0:T(4,128)} %rest.1) | copy-start | bytes 55300
  3.2 0.7 %copy-start.4 = (s32[3,512]{1,0:T(4,128)S(1)}, s32[3,512]{1,0:T(4,128)}, u32[]{:S(2)}) copy-start(s32[3,512]{1,0:T(4,128)} %base.1) | copy-start | bytes 18436
  3.9 0.7 %copy-start.5 = (f32[3,512]{1,0:T(4,128)S(1)}, f32[3,512]{1,0:T(4,128)}, u32[]{:S(2)}) copy-start(f32[3,512]{1,0:T(4,128)} %frac.1) | copy-start | bytes 18436
  4.6 37.2 %copy-start.1 = (f32[19,16,4,128]{3,2,1,0:T(4,128)S(1)}, f32[19,16,4,128]{3,2,1,0:T(4,128)}, u32[]{:S(2)}) copy-start(f32[19,16,4,128]{3,2,1,0:T(4,128)} %param.6) | copy-start | bytes 1867780
  5.9 17.2 %collective-permute-start.1 = (f32[400,128]{1,0:T(8,128)S(1)}, f32[400,128]{1,0:T(8,128)S(1)}, u32[]{:S(2)}, u32[]{:S(2)}) collective-permute-start(f32[400,128]{1,0:T(8,128)S(1)} %get-tuple-element.19), channel_id=1, source_target_pairs={{0,63},{1,0},{2,1},{3,2},{4,3},{5,4},{6,5},{7,6},{8,7},{9,8},{10,9... | collective-permute-start | bytes 614408 | tf_op jit(solution)/shard_map/ppermute | solution.py:371
  12.0 11.0 %collective-permute-start = (f32[336,128]{1,0:T(8,128)S(1)}, f32[336,128]{1,0:T(8,128)S(1)}, u32[]{:S(2)}, u32[]{:S(2)}) collective-permute-start(f32[336,128]{1,0:T(8,128)S(1)} %get-tuple-element.18), channel_id=1, source_target_pairs={{0,1},{1,2},{2,3},{3,4},{4,5},{5,6},{6,7},{7,8},{8,9},{9,10},{10,1... | collective-permute-start | bytes 516104 | tf_op jit(solution)/shard_map/ppermute | solution.py:371
  23.1 18.6 %collective-permute-start.3 = (f32[160,128]{1,0:T(8,128)S(1)}, f32[160,128]{1,0:T(8,128)S(1)}, u32[]{:S(2)}, u32[]{:S(2)}) collective-permute-start(f32[160,128]{1,0:T(8,128)S(1)} %get-tuple-element.22), channel_id=1, source_target_pairs={{0,960},{64,0},{128,64},{192,128},{256,192},{320,256},{384,320},{4... | collective-permute-start | bytes 245768 | tf_op jit(solution)/shard_map/ppermute | solution.py:371
  36.8 4.9 %collective-permute-start.2 = (f32[128,128]{1,0:T(8,128)S(1)}, f32[128,128]{1,0:T(8,128)S(1)}, u32[]{:S(2)}, u32[]{:S(2)}) collective-permute-start(f32[128,128]{1,0:T(8,128)S(1)} %get-tuple-element.21), channel_id=1, source_target_pairs={{0,64},{64,128},{128,192},{192,256},{256,320},{320,384},{384,448},... | collective-permute-start | bytes 196616 | tf_op jit(solution)/shard_map/ppermute | solution.py:371

commit v2 on v1

--- a/solution.py
+++ b/solution.py
@@ -42,11 +42,11 @@
 UP_X = [q for q in range(19) if lattice_speeds[q][0] == 1]
 DOWN_X = [q for q in range(19) if lattice_speeds[q][0] == -1]
 
-FORCE_ROWS = 9 * WX + 3 * 16
-UP_ROWS = FORCE_ROWS + 4 * WX + 5 * WX
-DOWN_ROWS = FORCE_ROWS + 8 * WX + 5 * WX
-RIGHT_ROWS = 3 * 24 + 32 + 24
-LEFT_ROWS = 3 * 24 + 2 * 32 + 24
+FORCE_ROWS = 9 * WX + 32
+POP_ROWS = FORCE_ROWS + 4 * WX
+BEHIND_ROWS = POP_ROWS + 5 * WX
+STRIP_ROWS = BEHIND_ROWS + WX
+SIDE_ROWS = 3 * 24 + 2 * 32 + 24
 
 
 def outer_weight(r):
@@ -71,11 +71,11 @@
     return lax.broadcasted_iota(jnp.int32, shape, dim)
 
 
-def edge_forces(base, frac, edges, stiffness, rest):
+def edge_forces(base, frac, edges, stiffness, rest, row):
     head = edges[0:1]
     tail = edges[1:2]
     run = head >> 7
-    local = iota((TILE, EDGES), 0)
+    local = jnp.concatenate([row] * (EDGES // NZ), axis=1)
     plus = local == (tail & (TILE - 1))
     minus = local == (head & (TILE - 1))
     signed = jnp.where(plus, 1.0, jnp.where(minus, -1.0, 0.0)).astype(bf16)
@@ -105,10 +105,31 @@
     return jnp.concatenate([-pulled[8 * t : 8 * t + 3] for t in range(4)], axis=1)
 
 
+def rows_kernel(row):
+    row[...] = iota((TILE, NZ), 0)
+
+
 def spread_kernel(
-    pop, base, frac, edges, stiffness, rest, force, moment, plane_out, high_out, low_out, edge_out, up, down
+    pop,
+    base,
+    frac,
+    edges,
+    stiffness,
+    rest,
+    row,
+    force,
+    moment,
+    plane_out,
+    high_out,
+    low_out,
+    edge_out,
+    even_strip,
+    odd_strip,
 ):
-    membrane = edge_forces(base[...], frac[...], edges[...], stiffness[...], rest[...])
+    springs = jnp.concatenate([stiffness[k : k + 1] for k in range(EDGES // NZ)], axis=1)
+    row = row[...]
+    membrane = edge_forces(base[...], frac[...], edges[...], springs, rest[...], row)
+    cell = base[...]
     part = frac[...]
     kernel = [
         outer_weight(1.0 + part),
@@ -116,7 +137,6 @@
         inner_weight(1.0 - part),
         outer_weight(2.0 - part),
     ]
-    cell = base[...]
 
     def columns(rows, offset, dim):
         total = jnp.zeros((rows, VERTS), f32)
@@ -136,6 +156,17 @@
     z_high, z_low = halves(along_z)
     high_out[...] = z_high
     low_out[...] = z_low
+
+    plane_high, plane_low = halves(plane)
+    for c in range(3):
+        load_high, load_low = halves(along_z * membrane[c : c + 1])
+        result = (
+            along_last(plane_high, load_high)
+            + along_last(plane_low, load_high)
+            + along_last(plane_high, load_low)
+        )
+        for y in range(SY):
+            force[(y * 3 + c) * SX : (y * 3 + c + 1) * SX] = result[y * SX : (y + 1) * SX]
 
     density = pop[0:CELLS]
     moments = [None, None, None]
@@ -153,49 +184,63 @@
     for d in range(3):
         moment[(d + 1) * CELLS : (d + 2) * CELLS] = moments[d]
 
-    plane_high, plane_low = halves(plane)
-    for c in range(3):
-        load_high, load_low = halves(along_z * membrane[c : c + 1])
-        result = (
-            along_last(plane_high, load_high)
-            + along_last(plane_low, load_high)
-            + along_last(plane_high, load_low)
-        )
-        for y in range(SY):
-            force[(y * 3 + c) * SX : (y * 3 + c + 1) * SX] = result[y * SX : (y + 1) * SX]
-
-    def strips(out, slab, rows, dirs, edge_row):
-        at = 0
+    def strip(out, slab, dirs, edge_row, behind):
         for k in range(9):
-            out[at : at + WX] = force[(slab * 3 + k) * SX : (slab * 3 + k) * SX + WX]
-            at += WX
-        for x in (16, 17, 23):
+            value = force[(slab * 3 + k) * SX : (slab * 3 + k) * SX + WX]
+            if behind is not None and k >= 6:
+                source = (k - 5) * CELLS + behind
+                value = value + 2.0 * moment[pl.ds(source, WX, stride=WY), :]
+            out[k * WX : (k + 1) * WX] = value
+        for n, x in enumerate((16, 17, 23)):
+            at = 9 * WX + 9 * n
             out[at : at + 9] = force[pl.ds(slab * 3 * SX + x, 9, stride=SX), :]
-            at += 16
-        for y in rows:
-            for q in range(4):
-                out[at : at + WX] = moment[pl.ds(q * CELLS + y, WX, stride=WY), :]
-                at += WX
-        for q in dirs:
+        for q in range(4):
+            at = FORCE_ROWS + q * WX
+            out[at : at + WX] = moment[pl.ds(q * CELLS + edge_row, WX, stride=WY), :]
+        for k, q in enumerate(dirs):
+            at = POP_ROWS + k * WX
             out[at : at + WX] = pop[pl.ds(q * CELLS + edge_row, WX, stride=WY), :]
-            at += WX
-
-    strips(up, 4, (3,), UP_Y, 3)
-    strips(down, 0, (0, 1), DOWN_Y, 0)
+        if behind is not None:
+            out[BEHIND_ROWS:STRIP_ROWS] = moment[pl.ds(behind, WX, stride=WY), :]
+
+    odd = lax.axis_index("gy") & 1
+
+    @pl.when(odd == 0)
+    def _():
+        strip(even_strip, 4, UP_Y, 3, None)
+        strip(odd_strip, 0, DOWN_Y, 0, 1)
+
+    @pl.when(odd == 1)
+    def _():
+        strip(odd_strip, 4, UP_Y, 3, None)
+        strip(even_strip, 0, DOWN_Y, 0, 1)
+
     for k, q in enumerate(UP_X):
         edge_out[k * 4 : k * 4 + 4] = pop[q * CELLS + 60 : q * CELLS + 64]
     for k, q in enumerate(DOWN_X):
         edge_out[24 + k * 4 : 24 + k * 4 + 4] = pop[q * CELLS : q * CELLS + 4]
 
 
-def merge_kernel(force_in, moment, edge, below, above, force, right, left):
+def merge_kernel(force_in, moment, edge, even_strip, odd_strip, force, right, left, below, above):
+    odd = lax.axis_index("gy") & 1
+
+    @pl.when(odd == 0)
+    def _():
+        below[...] = odd_strip[...]
+        above[...] = even_strip[...]
+
+    @pl.when(odd == 1)
+    def _():
+        below[...] = even_strip[...]
+        above[...] = odd_strip[...]
+
     def outer(block, slab):
         for k in range(9):
             row = (slab * 3 + k) * SX
             force[row : row + WX] = force_in[row : row + WX] + block[k * WX : k * WX + WX]
         for n, x in enumerate((16, 17, 23)):
             rows = pl.ds(slab * 3 * SX + x, 9, stride=SX)
-            at = 9 * WX + 16 * n
+            at = 9 * WX + 9 * n
             force[rows, :] = force_in[rows, :] + block[at : at + 9]
 
     for k in range(9, 12):
@@ -217,7 +262,8 @@
             for y in range(4):
                 out[at + 4 + y * 4 : at + 8 + y * 4] = moment[pl.ds(x * 4 + y, 4, stride=CELLS), :]
             out[at + 20 : at + 24] = above[pl.ds(FORCE_ROWS + x, 4, stride=WX), :]
-            out[at + 24 : at + 28] = above[pl.ds(FORCE_ROWS + 4 * WX + x, 4, stride=WX), :]
+            out[at + 24 : at + 25] = above[BEHIND_ROWS + x : BEHIND_ROWS + x + 1]
+            out[at + 25 : at + 28] = jnp.zeros((3, NZ), f32)
             at += 32
         x = columns[0]
         for k, q in enumerate(dirs):
@@ -226,11 +272,11 @@
             if step == 0:
                 out[at : at + 4] = edge[row : row + 4]
             elif step == 1:
-                source = FORCE_ROWS + 4 * WX + UP_Y.index(q) * WX + x
+                source = POP_ROWS + UP_Y.index(q) * WX + x
                 out[at : at + 1] = below[source : source + 1]
                 out[at + 1 : at + 4] = edge[row : row + 3]
             else:
-                source = FORCE_ROWS + 8 * WX + DOWN_Y.index(q) * WX + x
+                source = POP_ROWS + DOWN_Y.index(q) * WX + x
                 out[at : at + 3] = edge[row + 1 : row + 4]
                 out[at + 3 : at + 4] = above[source : source + 1]
             at += 4
@@ -257,9 +303,12 @@
                 value = below[FORCE_ROWS + q * WX : FORCE_ROWS + (q + 1) * WX]
             elif slab < 5:
                 value = moment[pl.ds(q * CELLS + slab - 1, WX, stride=WY), :]
+            elif slab == 5:
+                value = above[FORCE_ROWS + q * WX : FORCE_ROWS + (q + 1) * WX]
+            elif q == 0:
+                value = above[BEHIND_ROWS:STRIP_ROWS]
             else:
-                source = FORCE_ROWS + ((slab - 5) * 4 + q) * WX
-                value = above[source : source + WX]
+                value = jnp.zeros((WX, NZ), f32)
             ext[row : row + WX] = value
             ext[row + WX : row + SX] = jnp.ones((8, NZ), f32)
     ext[pl.ds(23, 28, stride=SX), :] = west[72 : 72 + 28]
@@ -298,10 +347,10 @@
             if 0 <= y_from <= 3:
                 value = pop[pl.ds(q * CELLS + y_from, WX, stride=WY), :]
             elif y_from < 0:
-                source = FORCE_ROWS + 4 * WX + UP_Y.index(q) * WX
+                source = POP_ROWS + UP_Y.index(q) * WX
                 value = below[source : source + WX]
             else:
-                source = FORCE_ROWS + 8 * WX + DOWN_Y.index(q) * WX
+                source = POP_ROWS + DOWN_Y.index(q) * WX
                 value = above[source : source + WX]
             if step_x == 1:
                 row = 104 + UP_X.index(q) * 4 + y_to
@@ -353,16 +402,16 @@
         sampled[c : c + 1] = jnp.sum(value * plane[...], axis=0, keepdims=True)
 
 
-def call(kernel, outputs, scratch, name, operands):
-    vmem = pl.BlockSpec(memory_space=pltpu.VMEM)
+def call(kernel, outputs, scratch, name, operands, cost=None):
     return pl.pallas_call(
         kernel,
         out_shape=[jax.ShapeDtypeStruct(shape, kind) for shape, kind in outputs],
-        in_specs=[vmem] * len(operands),
-        out_specs=[vmem] * len(outputs),
-        scratch_shapes=[pltpu.VMEM(shape, f32) for shape in scratch],
+        in_specs=[pl.BlockSpec(memory_space=pltpu.VMEM)] * len(operands),
+        out_specs=[pl.BlockSpec(memory_space=pltpu.VMEM)] * len(outputs),
+        scratch_shapes=scratch,
         compiler_params=pltpu.CompilerParams(vmem_limit_bytes=32 * 1024 * 1024),
         name=name,
+        cost_estimate=cost,
     )(*operands)
 
 
@@ -371,9 +420,19 @@
     return lax.ppermute(value, axis, [(i, (i + step) % size) for i in range(size)])
 
 
+def swap(value, axis, first):
+    size = lax.axis_size(axis)
+    pairs = []
+    for i in range(first, size + first, 2):
+        pairs += [(i % size, (i + 1) % size), ((i + 1) % size, i % size)]
+    return lax.ppermute(value, axis, pairs)
+
+
 def per_device(populations, vert_base, vert_frac, edges, stiffness, rest):
     pop = populations.reshape(19 * CELLS, NZ)
-    force, moment, plane, z_high, z_low, edge, up, down = call(
+    cost = pl.CostEstimate(flops=1 << 30, bytes_accessed=1 << 23, transcendentals=0)
+    (row,) = call(rows_kernel, [((TILE, NZ), jnp.int32)], [], "rows", [], cost)
+    force, moment, plane, z_high, z_low, edge, even_strip, odd_strip = call(
         spread_kernel,
         [
             ((SY * 3 * SX, NZ), f32),
@@ -382,28 +441,38 @@
             ((NZ, VERTS), bf16),
             ((NZ, VERTS), bf16),
             ((48, NZ), f32),
-            ((UP_ROWS, NZ), f32),
-            ((DOWN_ROWS, NZ), f32),
+            ((STRIP_ROWS, NZ), f32),
+            ((STRIP_ROWS, NZ), f32),
         ],
         [],
         "spread",
-        [pop, vert_base, vert_frac, edges, stiffness.reshape(1, EDGES), rest],
+        [pop, vert_base, vert_frac, edges, stiffness.reshape(EDGES // NZ, NZ), rest, row],
     )
-    below = shift(up, "gy", 1)
-    above = shift(down, "gy", -1)
-    force, right, left = call(
+    even_strip = swap(even_strip, "gy", 0)
+    odd_strip = swap(odd_strip, "gy", 1)
+    force, right, left, below, above = call(
         merge_kernel,
-        [((SY * 3 * SX, NZ), f32), ((RIGHT_ROWS, NZ), f32), ((LEFT_ROWS, NZ), f32)],
+        [
+            ((SY * 3 * SX, NZ), f32),
+            ((SIDE_ROWS, NZ), f32),
+            ((SIDE_ROWS, NZ), f32),
+            ((STRIP_ROWS, NZ), f32),
+            ((STRIP_ROWS, NZ), f32),
+        ],
         [],
         "merge",
-        [force, moment, edge, below, above],
+        [force, moment, edge, even_strip, odd_strip],
     )
     west = shift(right, "gx", 1)
     east = shift(left, "gx", -1)
     fresh, sampled = call(
         collide_kernel,
         [((19 * CELLS, NZ), f32), ((3, VERTS), f32)],
-        [(SY * 3 * SX, NZ), (SY * 4 * SX, NZ), (SY * 3 * SX, 2 * NZ)],
+        [
+            pltpu.VMEM((SY * 3 * SX, NZ), f32),
+            pltpu.VMEM((SY * 4 * SX, NZ), f32),
+            pltpu.VMEM((SY * 3 * SX, 2 * NZ), f32),
+        ],
         "collide",
         [pop, force, moment, below, above, west, east, plane, z_high, z_low],
     )

time: 43.8 us -> 35.4 us (0.81)
  waiting for transfers between devices: 14 us -> 7.45 us
  local copies, waits for them, and re-layouts: 3.92 us -> 1.04 us
  starting transfers between devices: 21.7 us -> 23 us
    ppermute x4 -> x2, waiting for transfers between devices: 14 us -> 2.1 us  [shift(): lax.ppermute(value, axis, [(i, (i + step) % size) for i in range(size)])]
    ppermute x0 -> x2, starting transfers between devices: none -> 9.28 us  [swap(): return lax.ppermute(value, axis, pairs)]
    ppermute x4 -> x2, starting transfers between devices: 21.7 us -> 13.7 us  [shift(): lax.ppermute(value, axis, [(i, (i + step) % size) for i in range(size)])]
    ppermute x0 -> x2, waiting for transfers between devices: none -> 5.35 us  [swap(): return lax.ppermute(value, axis, pairs)]
    unnamed x12, local copies, waits for them, and re-layouts: 3.21 us -> 1.04 us
    reshape x1 -> x0, local copies, waits for them, and re-layouts: 0.71 us -> none  [per_device(): stiffness.reshape(1, EDGES)]
    pallas_call x3 -> x4, Pallas kernels: 3.02 us -> 3.05 us  [call(): pl.pallas_call(kernel, out_shape=[jax.ShapeDtypeStruct(shape, kind) for s...]
where the time goes in v2:
time: 35.4 us; the launch traced here: 35.2 us
  starting transfers between devices  23 us (65%)
  waiting for transfers between devices  7.45 us (21%)
  Pallas kernels  3.05 us (9%)
  local copies, waits for them, and re-layouts  1.04 us (3%)
  between operations  0.74 us (2%)
    ppermute x2, starting transfers between devices, shift(): lax.ppermute(value, axis, [(i, (i + step) % size) for i in range(size)])  13.7 us
    ppermute x2, starting transfers between devices, swap(): return lax.ppermute(value, axis, pairs)  9.28 us
    ppermute x2, waiting for transfers between devices, swap(): return lax.ppermute(value, axis, pairs)  5.35 us
    pallas_call x4, Pallas kernels, call(): pl.pallas_call(kernel, out_shape=[jax.ShapeDtypeStruct(shape, kind) for s...  3.05 us
    ppermute x2, waiting for transfers between devices, shift(): lax.ppermute(value, axis, [(i, (i + step) % size) for i in range(size)])  2.1 us
    unnamed x12, local copies, waits for them, and re-layouts  1.04 us
  transfers between devices with their start and end apart: 4, of which 2 were waited for; matrix products, arithmetic and copies ran while one was open for 0% of the time, Pallas kernels for 0%

profile of v2, /device:TPU:8, one launch (start us, length us, event | category | flops | bytes accessed | tf_op | source)
XLA Modules:
  0.0 35.2 jit_solution(14978352622953917409)
XLA Ops:
  0.6 0.0 copy-start.1
  0.6 0.0 copy-start
  0.7 0.0 copy-start.2
  0.7 0.0 copy-start.3
  0.7 0.0 copy-start.4
  0.7 0.0 copy-start.5
  0.7 0.7 %copy-done.1 = f32[3,1536]{1,0:T(4,128)S(1)} copy-done((f32[3,1536]{1,0:T(4,128)S(1)}, f32[3,1536]{1,0:T(4,128)}, u32[]{:S(2)}) %copy-start.1) | copy-done | bytes 18456
  1.4 0.4 %copy-done = f32[19,16,4,128]{3,2,1,0:T(4,128)S(1)} copy-done((f32[19,16,4,128]{3,2,1,0:T(4,128)S(1)}, f32[19,16,4,128]{3,2,1,0:T(4,128)}, u32[]{:S(2)}) %copy-start) | copy-done | bytes 622616
  1.7 0.0 copy-done.2
  1.7 0.0 copy-done.3
  1.7 0.0 copy-done.4
  1.7 0.0 copy-done.5
  1.7 1.3 %spread.1 = (f32[504,128]{1,0:T(8,128)S(1)}, f32[256,128]{1,0:T(8,128)S(1)}, f32[168,512]{1,0:T(8,128)S(1)}, bf16[128,512]{1,0:T(8,128)(2,1)S(1)}, bf16[128,512]...) custom-call(f32[1216,128]{1,0:T(8,128)S(1)} %bitcast.3, ...), custom_call_target="tpu_custom_call" | custom-call | tf_op jit(solution)/shard_map/spread/pallas_call | solution.py:406
  3.1 3.6 %collective-permute-start = (f32[336,128]{1,0:T(8,128)S(1)}, f32[336,128]{1,0:T(8,128)S(1)}, u32[]{:S(2)}, u32[]{:S(2)}) collective-permute-start(f32[336,128]{1,0:T(8,128)S(1)} %get-tuple-element.20), channel_id=1, source_target_pairs={{0,1},{1,0},{2,3},{3,2},{4,5},{5,4},{6,7},{7,6},{8,9},{9,8},{10,11... | collective-permute-start | bytes 516104 | tf_op jit(solution)/shard_map/ppermute | solution.py:428
  6.7 5.7 %collective-permute-start.1 = (f32[336,128]{1,0:T(8,128)S(1)}, f32[336,128]{1,0:T(8,128)S(1)}, u32[]{:S(2)}, u32[]{:S(2)}) collective-permute-start(f32[336,128]{1,0:T(8,128)S(1)} %get-tuple-element.21), channel_id=1, source_target_pairs={{1,2},{2,1},{3,4},{4,3},{5,6},{6,5},{7,8},{8,7},{9,10},{10,9},{11,... | collective-permute-start | bytes 516104 | tf_op jit(solution)/shard_map/ppermute | solution.py:428
  12.4 0.0 collective-permute-done.even_strip
  12.4 5.3 %collective-permute-done.1.odd_strip = f32[336,128]{1,0:T(8,128)S(1)} collective-permute-done((f32[336,128]{1,0:T(8,128)S(1)}, f32[336,128]{1,0:T(8,128)S(1)}, u32[]{:S(2)}, u32[]{:S(2)}) %collective-permute-start.1) | collective-permute-done | bytes 172064 | tf_op jit(solution)/shard_map/ppermute | solution.py:428
  17.7 0.1 merge.1
  17.8 0.0 collective-permute-start.2
  17.8 13.7 %collective-permute-start.3 = (f32[160,128]{1,0:T(8,128)S(1)}, f32[160,128]{1,0:T(8,128)S(1)}, u32[]{:S(2)}, u32[]{:S(2)}) collective-permute-start(f32[160,128]{1,0:T(8,128)S(1)} %get-tuple-element.26), channel_id=1, source_target_pairs={{0,960},{64,0},{128,64},{192,128},{256,192},{320,256},{384,320},{4... | collective-permute-start | bytes 245768 | tf_op jit(solution)/shard_map/ppermute | solution.py:420
  31.5 2.1 %collective-permute-done.2.west = f32[160,128]{1,0:T(8,128)S(1)} collective-permute-done((f32[160,128]{1,0:T(8,128)S(1)}, f32[160,128]{1,0:T(8,128)S(1)}, u32[]{:S(2)}, u32[]{:S(2)}) %collective-permute-start.2) | collective-permute-done | bytes 81952 | tf_op jit(solution)/shard_map/ppermute | solution.py:420
  33.6 0.0 collective-permute-done.3.east
  33.6 1.6 %collide.1 = (f32[1216,128]{1,0:T(8,128)}, f32[3,512]{1,0:T(4,128)}) custom-call(f32[1216,128]{1,0:T(8,128)S(1)} %bitcast.4, f32[504,128]{1,0:T(8,128)S(1)} %get-tuple-element.22.force_in, f32[256,128]{1,0:T(8,128)S(1)} %get-tuple-element.18.moment, f32[336,128]{1,0:T(8,128)S(1)} %get-tuple-element.23.below, f32[336,128]{1,0:T(8,128)S(1)} %get-tuple-element.24.above, ...), custom_call_target="tpu_custom_call" | custom-call | tf_op jit(solution)/shard_map/collide/pallas_call | solution.py:406
  (1 shorter events, 0.0 us)
Async XLA Ops:
  0.6 0.7 %copy-start.1 = (f32[3,1536]{1,0:T(4,128)S(1)}, f32[3,1536]{1,0:T(4,128)}, u32[]{:S(2)}) copy-start(f32[3,1536]{1,0:T(4,128)} %rest.1) | copy-start | bytes 55300
  0.6 1.1 %copy-start = (f32[19,16,4,128]{3,2,1,0:T(4,128)S(1)}, f32[19,16,4,128]{3,2,1,0:T(4,128)}, u32[]{:S(2)}) copy-start(f32[19,16,4,128]{3,2,1,0:T(4,128)} %param.6) | copy-start | bytes 1867780
  0.7 1.1 %copy-start.2 = (s32[2,1536]{1,0:T(2,128)S(1)}, s32[2,1536]{1,0:T(2,128)}, u32[]{:S(2)}) copy-start(s32[2,1536]{1,0:T(2,128)} %edges.1) | copy-start | bytes 36868
  0.7 1.1 %copy-start.3 = (s32[3,512]{1,0:T(4,128)S(1)}, s32[3,512]{1,0:T(4,128)}, u32[]{:S(2)}) copy-start(s32[3,512]{1,0:T(4,128)} %base.1) | copy-start | bytes 18436
  0.7 1.1 %copy-start.4 = (f32[3,512]{1,0:T(4,128)S(1)}, f32[3,512]{1,0:T(4,128)}, u32[]{:S(2)}) copy-start(f32[3,512]{1,0:T(4,128)} %frac.1) | copy-start | bytes 18436
  0.7 1.1 %copy-start.5 = (f32[1536]{0:T(1024)S(1)}, f32[1536]{0:T(1024)}, u32[]{:S(2)}) copy-start(f32[1536]{0:T(1024)} %param.10) | copy-start | bytes 18436
  3.1 9.3 %collective-permute-start = (f32[336,128]{1,0:T(8,128)S(1)}, f32[336,128]{1,0:T(8,128)S(1)}, u32[]{:S(2)}, u32[]{:S(2)}) collective-permute-start(f32[336,128]{1,0:T(8,128)S(1)} %get-tuple-element.20), channel_id=1, source_target_pairs={{0,1},{1,0},{2,3},{3,2},{4,5},{5,4},{6,7},{7,6},{8,9},{9,8},{10,11... | collective-permute-start | bytes 516104 | tf_op jit(solution)/shard_map/ppermute | solution.py:428
  6.7 11.1 %collective-permute-start.1 = (f32[336,128]{1,0:T(8,128)S(1)}, f32[336,128]{1,0:T(8,128)S(1)}, u32[]{:S(2)}, u32[]{:S(2)}) collective-permute-start(f32[336,128]{1,0:T(8,128)S(1)} %get-tuple-element.21), channel_id=1, source_target_pairs={{1,2},{2,1},{3,4},{4,3},{5,6},{6,5},{7,8},{8,7},{9,10},{10,9},{11,... | collective-permute-start | bytes 516104 | tf_op jit(solution)/shard_map/ppermute | solution.py:428
  17.8 15.8 %collective-permute-start.2 = (f32[160,128]{1,0:T(8,128)S(1)}, f32[160,128]{1,0:T(8,128)S(1)}, u32[]{:S(2)}, u32[]{:S(2)}) collective-permute-start(f32[160,128]{1,0:T(8,128)S(1)} %get-tuple-element.25), channel_id=1, source_target_pairs={{0,64},{64,128},{128,192},{192,256},{256,320},{320,384},{384,448},... | collective-permute-start | bytes 245768 | tf_op jit(solution)/shard_map/ppermute | solution.py:420
  17.8 15.8 %collective-permute-start.3 = (f32[160,128]{1,0:T(8,128)S(1)}, f32[160,128]{1,0:T(8,128)S(1)}, u32[]{:S(2)}, u32[]{:S(2)}) collective-permute-start(f32[160,128]{1,0:T(8,128)S(1)} %get-tuple-element.26), channel_id=1, source_target_pairs={{0,960},{64,0},{128,64},{192,128},{256,192},{320,256},{384,320},{4... | collective-permute-start | bytes 245768 | tf_op jit(solution)/shard_map/ppermute | solution.py:420

commit v3 on v2

--- a/solution.py
+++ b/solution.py
@@ -42,10 +42,11 @@
 UP_X = [q for q in range(19) if lattice_speeds[q][0] == 1]
 DOWN_X = [q for q in range(19) if lattice_speeds[q][0] == -1]
 
-FORCE_ROWS = 9 * WX + 32
+FORCE_ROWS = 64
+MARK_ROW = 57
 POP_ROWS = FORCE_ROWS + 4 * WX
-BEHIND_ROWS = POP_ROWS + 5 * WX
-STRIP_ROWS = BEHIND_ROWS + WX
+UP_ROWS = POP_ROWS + 5 * WX
+STRIP_ROWS = UP_ROWS + 4 * WX
 SIDE_ROWS = 3 * 24 + 2 * 32 + 24
 
 
@@ -109,6 +110,48 @@
     row[...] = iota((TILE, NZ), 0)
 
 
+def kernel_of(frac):
+    return [
+        outer_weight(1.0 + frac),
+        inner_weight(frac),
+        inner_weight(1.0 - frac),
+        outer_weight(2.0 - frac),
+    ]
+
+
+def columns(kernel, offset):
+    total = jnp.where(offset == 0, kernel[0], 0.0)
+    for step in range(1, 4):
+        total = jnp.where(offset == step, kernel[step], total)
+    return total
+
+
+def windows(lanes, marks):
+    component = (iota((1, TILE), 1) >> 3) & 3
+    depth = iota((NZ, TILE), 0).astype(f32)
+    match = jnp.where(depth == marks, 1.0, 0.0)
+    spots = jnp.concatenate([jnp.where(component == c, match, 0.0) for c in range(3)], axis=0)
+    high, low = halves(lanes)
+    rows = lanes.shape[0]
+    both = jnp.concatenate([high.astype(f32), low.astype(f32)], axis=0).astype(bf16)
+    wide = along_last(both, spots.astype(bf16))
+    return wide[0:rows] + wide[rows : 2 * rows]
+
+
+def strip(out, lanes, marks, moment, pop, slab, dirs, edge_row):
+    for k in range(3):
+        out[k * WX : (k + 1) * WX] = lanes[(slab + k) * SX : (slab + k) * SX + WX]
+    for n, x in enumerate((16, 17, 23)):
+        out[48 + 3 * n : 51 + 3 * n] = lanes[pl.ds(slab * SX + x, 3, stride=SX), :]
+    out[MARK_ROW:FORCE_ROWS] = jnp.broadcast_to(marks[0:1], (FORCE_ROWS - MARK_ROW, NZ))
+    for q in range(4):
+        at = FORCE_ROWS + q * WX
+        out[at : at + WX] = moment[pl.ds(q * CELLS + edge_row, WX, stride=WY), :]
+    for k, q in enumerate(dirs):
+        at = POP_ROWS + k * WX
+        out[at : at + WX] = pop[pl.ds(q * CELLS + edge_row, WX, stride=WY), :]
+
+
 def spread_kernel(
     pop,
     base,
@@ -117,56 +160,53 @@
     stiffness,
     rest,
     row,
-    force,
+    lanes,
+    marks,
+    plane_out,
     moment,
-    plane_out,
-    high_out,
-    low_out,
     edge_out,
-    even_strip,
-    odd_strip,
+    up,
+    down,
 ):
     springs = jnp.concatenate([stiffness[k : k + 1] for k in range(EDGES // NZ)], axis=1)
-    row = row[...]
-    membrane = edge_forces(base[...], frac[...], edges[...], springs, rest[...], row)
+    membrane = edge_forces(base[...], frac[...], edges[...], springs, rest[...], row[...])
+    part = frac[...]
+    kernel = kernel_of(part)
     cell = base[...]
-    part = frac[...]
-    kernel = [
-        outer_weight(1.0 + part),
-        inner_weight(part),
-        inner_weight(1.0 - part),
-        outer_weight(2.0 - part),
-    ]
-
-    def columns(rows, offset, dim):
-        total = jnp.zeros((rows, VERTS), f32)
-        for step in range(4):
-            total = jnp.where(offset == step, kernel[step][dim : dim + 1], total)
-        return total
 
     slot = iota((SX, VERTS), 0)
     slot = jnp.where(slot == SX - 1, -1, slot)
-    along_x = columns(SX, slot - (cell[0:1] & (WX - 1)) + 1, 0)
+    along_x = columns([k[0:1] for k in kernel], slot - (cell[0:1] & (WX - 1)) + 1)
     slab = iota((8, VERTS), 0)
-    along_y = columns(8, slab - (cell[1:2] & (WY - 1)), 1)
-    depth = iota((NZ, VERTS), 0)
-    along_z = columns(NZ, (depth - cell[2:3] + 1) & (NZ - 1), 2)
+    along_y = columns([k[1:2] for k in kernel], slab - (cell[1:2] & (WY - 1)))
     plane = jnp.concatenate([along_x * along_y[y : y + 1] for y in range(SY)], axis=0)
     plane_out[...] = plane
-    z_high, z_low = halves(along_z)
-    high_out[...] = z_high
-    low_out[...] = z_low
-
+
+    layer = iota((8, TILE), 0)
+    lane = iota((1, TILE), 1)
+    mark = jnp.zeros((1, TILE), jnp.int32)
+    blocks = []
+    for t in range(4):
+        span = slice(t * TILE, (t + 1) * TILE)
+        z = cell[2:3, span]
+        apart = ((z - z[:, 0:1] + 64) & (NZ - 1)) - 64
+        lowest = jnp.min(apart.astype(f32), axis=1, keepdims=True).astype(jnp.int32)
+        along_z = columns([k[2:3, span] for k in kernel], layer - apart + lowest)
+        start = z[:, 0:1] + lowest - 1
+        mark = jnp.where(lane >> 5 == t, (start + (lane & 7)) & (NZ - 1), mark)
+        block = [along_z * membrane[c : c + 1, span] for c in range(3)] + [jnp.zeros((8, TILE), f32)]
+        row_of = [jnp.zeros((32, TILE), f32)] * 4
+        row_of[t] = jnp.concatenate(block, axis=0)
+        blocks.append(jnp.concatenate(row_of, axis=1))
+    loaded = jnp.concatenate(blocks, axis=0)
+    marks[...] = jnp.broadcast_to(mark.astype(f32), (8, TILE))
     plane_high, plane_low = halves(plane)
-    for c in range(3):
-        load_high, load_low = halves(along_z * membrane[c : c + 1])
-        result = (
-            along_last(plane_high, load_high)
-            + along_last(plane_low, load_high)
-            + along_last(plane_high, load_low)
-        )
-        for y in range(SY):
-            force[(y * 3 + c) * SX : (y * 3 + c + 1) * SX] = result[y * SX : (y + 1) * SX]
+    load_high, load_low = halves(loaded)
+    lanes[...] = (
+        along_last(plane_high, load_high)
+        + along_last(plane_low, load_high)
+        + along_last(plane_high, load_low)
+    )
 
     density = pop[0:CELLS]
     moments = [None, None, None]
@@ -183,106 +223,75 @@
     moment[0:CELLS] = density
     for d in range(3):
         moment[(d + 1) * CELLS : (d + 2) * CELLS] = moments[d]
-
-    def strip(out, slab, dirs, edge_row, behind):
-        for k in range(9):
-            value = force[(slab * 3 + k) * SX : (slab * 3 + k) * SX + WX]
-            if behind is not None and k >= 6:
-                source = (k - 5) * CELLS + behind
-                value = value + 2.0 * moment[pl.ds(source, WX, stride=WY), :]
-            out[k * WX : (k + 1) * WX] = value
-        for n, x in enumerate((16, 17, 23)):
-            at = 9 * WX + 9 * n
-            out[at : at + 9] = force[pl.ds(slab * 3 * SX + x, 9, stride=SX), :]
-        for q in range(4):
-            at = FORCE_ROWS + q * WX
-            out[at : at + WX] = moment[pl.ds(q * CELLS + edge_row, WX, stride=WY), :]
-        for k, q in enumerate(dirs):
-            at = POP_ROWS + k * WX
-            out[at : at + WX] = pop[pl.ds(q * CELLS + edge_row, WX, stride=WY), :]
-        if behind is not None:
-            out[BEHIND_ROWS:STRIP_ROWS] = moment[pl.ds(behind, WX, stride=WY), :]
-
-    odd = lax.axis_index("gy") & 1
-
-    @pl.when(odd == 0)
-    def _():
-        strip(even_strip, 4, UP_Y, 3, None)
-        strip(odd_strip, 0, DOWN_Y, 0, 1)
-
-    @pl.when(odd == 1)
-    def _():
-        strip(odd_strip, 4, UP_Y, 3, None)
-        strip(even_strip, 0, DOWN_Y, 0, 1)
-
+    strip(up, lanes, marks, moment, pop, 4, UP_Y, 3)
+    strip(down, lanes, marks, moment, pop, 0, DOWN_Y, 0)
+    for q in range(4):
+        at = UP_ROWS + q * WX
+        down[at : at + WX] = moment[pl.ds(q * CELLS + 1, WX, stride=WY), :]
     for k, q in enumerate(UP_X):
         edge_out[k * 4 : k * 4 + 4] = pop[q * CELLS + 60 : q * CELLS + 64]
     for k, q in enumerate(DOWN_X):
         edge_out[24 + k * 4 : 24 + k * 4 + 4] = pop[q * CELLS : q * CELLS + 4]
 
 
-def merge_kernel(force_in, moment, edge, even_strip, odd_strip, force, right, left, below, above):
-    odd = lax.axis_index("gy") & 1
-
-    @pl.when(odd == 0)
-    def _():
-        below[...] = odd_strip[...]
-        above[...] = even_strip[...]
-
-    @pl.when(odd == 1)
-    def _():
-        below[...] = even_strip[...]
-        above[...] = odd_strip[...]
-
-    def outer(block, slab):
-        for k in range(9):
-            row = (slab * 3 + k) * SX
-            force[row : row + WX] = force_in[row : row + WX] + block[k * WX : k * WX + WX]
-        for n, x in enumerate((16, 17, 23)):
-            rows = pl.ds(slab * 3 * SX + x, 9, stride=SX)
-            at = 9 * WX + 9 * n
-            force[rows, :] = force_in[rows, :] + block[at : at + 9]
-
-    for k in range(9, 12):
-        force[k * SX : (k + 1) * SX] = force_in[k * SX : (k + 1) * SX]
-    for slab in (0, 4):
-        for k in range(9):
-            row = (slab * 3 + k) * SX + 16
-            force[row : row + 8] = force_in[row : row + 8]
-    outer(below, 0)
-    outer(above, 4)
-
-    def outgoing(out, sources, columns, offset, dirs):
-        at = 0
-        for x in sources:
-            out[at : at + 21] = force[pl.ds(x, 21, stride=SX), :]
-            at += 24
-        for x in columns:
-            out[at : at + 4] = below[pl.ds(FORCE_ROWS + x, 4, stride=WX), :]
-            for y in range(4):
-                out[at + 4 + y * 4 : at + 8 + y * 4] = moment[pl.ds(x * 4 + y, 4, stride=CELLS), :]
-            out[at + 20 : at + 24] = above[pl.ds(FORCE_ROWS + x, 4, stride=WX), :]
-            out[at + 24 : at + 25] = above[BEHIND_ROWS + x : BEHIND_ROWS + x + 1]
-            out[at + 25 : at + 28] = jnp.zeros((3, NZ), f32)
-            at += 32
-        x = columns[0]
-        for k, q in enumerate(dirs):
-            row = offset + k * 4
-            step = lattice_speeds[q][1]
-            if step == 0:
-                out[at : at + 4] = edge[row : row + 4]
-            elif step == 1:
-                source = POP_ROWS + UP_Y.index(q) * WX + x
-                out[at : at + 1] = below[source : source + 1]
-                out[at + 1 : at + 4] = edge[row : row + 3]
-            else:
-                source = POP_ROWS + DOWN_Y.index(q) * WX + x
-                out[at : at + 3] = edge[row + 1 : row + 4]
-                out[at + 3 : at + 4] = above[source : source + 1]
-            at += 4
-
-    outgoing(right, (15, 16, 17), (15,), 0, UP_X)
-    outgoing(left, (23, 0, 1), (0, 1), 24, DOWN_X)
+def tables_kernel(base, frac, lanes, marks, force, high_out, low_out):
+    wide = windows(lanes[...], marks[0:1])
+    for slab in range(SY):
+        for c in range(3):
+            row = (slab * 3 + c) * SX
+            force[row : row + SX] = wide[slab * SX : (slab + 1) * SX, c * NZ : (c + 1) * NZ]
+    kernel = kernel_of(frac[2:3])
+    depth = iota((NZ, VERTS), 0)
+    along_z = columns(kernel, (depth - base[2:3] + 1) & (NZ - 1))
+    z_high, z_low = halves(along_z)
+    high_out[...] = z_high
+    low_out[...] = z_low
+
+
+def outgoing(out, force, moment, edge, below, above, sources, spots, offset, dirs):
+    at = 0
+    for x in sources:
+        out[at : at + 21] = force[pl.ds(x, 21, stride=SX), :]
+        at += 24
+    for x in spots:
+        out[at : at + 4] = below[pl.ds(FORCE_ROWS + x, 4, stride=WX), :]
+        for y in range(4):
+            out[at + 4 + y * 4 : at + 8 + y * 4] = moment[pl.ds(x * 4 + y, 4, stride=CELLS), :]
+        out[at + 20 : at + 24] = above[pl.ds(FORCE_ROWS + x, 4, stride=WX), :]
+        out[at + 24 : at + 28] = above[pl.ds(UP_ROWS + x, 4, stride=WX), :]
+        at += 32
+    x = spots[0]
+    for k, q in enumerate(dirs):
+        row = offset + k * 4
+        step = lattice_speeds[q][1]
+        if step == 0:
+            out[at : at + 4] = edge[row : row + 4]
+        elif step == 1:
+            source = POP_ROWS + UP_Y.index(q) * WX + x
+            out[at : at + 1] = below[source : source + 1]
+            out[at + 1 : at + 4] = edge[row : row + 3]
+        else:
+            source = POP_ROWS + DOWN_Y.index(q) * WX + x
+            out[at : at + 3] = edge[row + 1 : row + 4]
+            out[at + 3 : at + 4] = above[source : source + 1]
+        at += 4
+
+
+def merge_kernel(force_in, moment, edge, below, above, force, right, left):
+    for row in range(0, SY * 3 * SX, SX):
+        force[row : row + SX] = force_in[row : row + SX]
+    for block, slab in ((below, 0), (above, 4)):
+        wide = windows(block[0:FORCE_ROWS], block[MARK_ROW : MARK_ROW + 1])
+        for c in range(3):
+            part = wide[:, c * NZ : (c + 1) * NZ]
+            for k in range(3):
+                row = ((slab + k) * 3 + c) * SX
+                force[row : row + WX] = force[row : row + WX] + part[k * WX : (k + 1) * WX]
+            for n, x in enumerate((16, 17, 23)):
+                rows = pl.ds((slab * 3 + c) * SX + x, 3, stride=3 * SX)
+                force[rows, :] = force[rows, :] + part[48 + 3 * n : 51 + 3 * n]
+    outgoing(right, force, moment, edge, below, above, (15, 16, 17), (15,), 0, UP_X)
+    outgoing(left, force, moment, edge, below, above, (23, 0, 1), (0, 1), 24, DOWN_X)
 
 
 def collide_kernel(
@@ -305,10 +314,8 @@
                 value = moment[pl.ds(q * CELLS + slab - 1, WX, stride=WY), :]
             elif slab == 5:
                 value = above[FORCE_ROWS + q * WX : FORCE_ROWS + (q + 1) * WX]
-            elif q == 0:
-                value = above[BEHIND_ROWS:STRIP_ROWS]
             else:
-                value = jnp.zeros((WX, NZ), f32)
+                value = above[UP_ROWS + q * WX : UP_ROWS + (q + 1) * WX]
             ext[row : row + WX] = value
             ext[row + WX : row + SX] = jnp.ones((8, NZ), f32)
     ext[pl.ds(23, 28, stride=SX), :] = west[72 : 72 + 28]
@@ -420,26 +427,17 @@
     return lax.ppermute(value, axis, [(i, (i + step) % size) for i in range(size)])
 
 
-def swap(value, axis, first):
-    size = lax.axis_size(axis)
-    pairs = []
-    for i in range(first, size + first, 2):
-        pairs += [(i % size, (i + 1) % size), ((i + 1) % size, i % size)]
-    return lax.ppermute(value, axis, pairs)
-
-
 def per_device(populations, vert_base, vert_frac, edges, stiffness, rest):
     pop = populations.reshape(19 * CELLS, NZ)
     cost = pl.CostEstimate(flops=1 << 30, bytes_accessed=1 << 23, transcendentals=0)
     (row,) = call(rows_kernel, [((TILE, NZ), jnp.int32)], [], "rows", [], cost)
-    force, moment, plane, z_high, z_low, edge, even_strip, odd_strip = call(
+    lanes, marks, plane, moment, edge, up, down = call(
         spread_kernel,
         [
-            ((SY * 3 * SX, NZ), f32),
+            ((SY * SX, NZ), f32),
+            ((8, NZ), f32),
+            ((SY * SX, VERTS), f32),
             ((4 * CELLS, NZ), f32),
-            ((SY * SX, VERTS), f32),
-            ((NZ, VERTS), bf16),
-            ((NZ, VERTS), bf16),
             ((48, NZ), f32),
             ((STRIP_ROWS, NZ), f32),
             ((STRIP_ROWS, NZ), f32),
@@ -448,20 +446,22 @@
         "spread",
         [pop, vert_base, vert_frac, edges, stiffness.reshape(EDGES // NZ, NZ), rest, row],
     )
-    even_strip = swap(even_strip, "gy", 0)
-    odd_strip = swap(odd_strip, "gy", 1)
-    force, right, left, below, above = call(
+    below = shift(up, "gy", 1)
+    above = shift(down, "gy", -1)
+    force, z_high, z_low = call(
+        tables_kernel,
+        [((SY * 3 * SX, NZ), f32), ((NZ, VERTS), bf16), ((NZ, VERTS), bf16)],
+        [],
+        "tables",
+        [vert_base, vert_frac, lanes, marks],
+        cost,
+    )
+    force, right, left = call(
         merge_kernel,
-        [
-            ((SY * 3 * SX, NZ), f32),
-            ((SIDE_ROWS, NZ), f32),
-            ((SIDE_ROWS, NZ), f32),
-            ((STRIP_ROWS, NZ), f32),
-            ((STRIP_ROWS, NZ), f32),
-        ],
+        [((SY * 3 * SX, NZ), f32), ((SIDE_ROWS, NZ), f32), ((SIDE_ROWS, NZ), f32)],
         [],
         "merge",
-        [force, moment, edge, even_strip, odd_strip],
+        [force, moment, edge, below, above],
     )
     west = shift(right, "gx", 1)
     east = shift(left, "gx", -1)

time: 35.4 us -> 33.9 us (0.958)
  the two profiles are of different devices: /device:TPU:8 before, /device:TPU:118 now
where the time goes in v3:
time: 33.9 us; the launch traced here: 33.7 us
  starting transfers between devices  19.5 us (58%)
  waiting for transfers between devices  9.25 us (27%)
  Pallas kernels  3.14 us (9%)
  local copies, waits for them, and re-layouts  1.04 us (3%)
  between operations  0.73 us (2%)
    ppermute x4, starting transfers between devices, shift(): lax.ppermute(value, axis, [(i, (i + step) % size) for i in range(size)])  19.5 us
    ppermute x4, waiting for transfers between devices, shift(): lax.ppermute(value, axis, [(i, (i + step) % size) for i in range(size)])  9.25 us
    pallas_call x5, Pallas kernels, call(): pl.pallas_call(kernel, out_shape=[jax.ShapeDtypeStruct(shape, kind) for s...  3.14 us
    unnamed x12, local copies, waits for them, and re-layouts  1.04 us
  transfers between devices with their start and end apart: 4, of which 3 were waited for; matrix products, arithmetic and copies ran while one was open for 0% of the time, Pallas kernels for 1%

profile of v3, /device:TPU:118, one launch (start us, length us, event | category | flops | bytes accessed | tf_op | source)
XLA Modules:
  0.0 33.7 jit_solution(12131361355042406858)
XLA Ops:
  0.6 0.0 copy-start.1
  0.6 0.0 copy-start
  0.7 0.0 copy-start.2
  0.7 0.0 copy-start.3
  0.7 0.0 copy-start.4
  0.7 0.0 copy-start.5
  0.7 0.7 %copy-done.1 = f32[3,1536]{1,0:T(4,128)S(1)} copy-done((f32[3,1536]{1,0:T(4,128)S(1)}, f32[3,1536]{1,0:T(4,128)}, u32[]{:S(2)}) %copy-start.1) | copy-done | bytes 18456
  1.4 0.4 %copy-done = f32[19,16,4,128]{3,2,1,0:T(4,128)S(1)} copy-done((f32[19,16,4,128]{3,2,1,0:T(4,128)S(1)}, f32[19,16,4,128]{3,2,1,0:T(4,128)}, u32[]{:S(2)}) %copy-start) | copy-done | bytes 622616
  1.7 0.0 copy-done.2
  1.7 0.0 copy-done.3
  1.7 0.0 copy-done.4
  1.7 0.0 copy-done.5
  1.7 0.9 %spread.1 = (f32[168,128]{1,0:T(8,128)S(1)}, f32[8,128]{1,0:T(8,128)S(1)}, f32[168,512]{1,0:T(8,128)S(1)}, f32[256,128]{1,0:T(8,128)S(1)}, f32[48,128]{1,0:T(8,1...) custom-call(f32[1216,128]{1,0:T(8,128)S(1)} %bitcast.3, s32[3,512]{1,0:T(4,128)S(1)} %copy-done.4, ...), custom_call_target="tpu_custom_call" | custom-call | tf_op jit(solution)/shard_map/spread/pallas_call | solution.py:413
  2.6 3.0 %collective-permute-start = (f32[272,128]{1,0:T(8,128)S(1)}, f32[272,128]{1,0:T(8,128)S(1)}, u32[]{:S(2)}, u32[]{:S(2)}) collective-permute-start(f32[272,128]{1,0:T(8,128)S(1)} %get-tuple-element.22), channel_id=1, source_target_pairs={{0,1},{1,2},{2,3},{3,4},{4,5},{5,6},{6,7},{7,8},{8,9},{9,10},{10,1... | collective-permute-start | bytes 417800 | tf_op jit(solution)/shard_map/ppermute | solution.py:427
  5.7 2.8 %collective-permute-start.1 = (f32[272,128]{1,0:T(8,128)S(1)}, f32[272,128]{1,0:T(8,128)S(1)}, u32[]{:S(2)}, u32[]{:S(2)}) collective-permute-start(f32[272,128]{1,0:T(8,128)S(1)} %get-tuple-element.23), channel_id=1, source_target_pairs={{0,63},{1,0},{2,1},{3,2},{4,3},{5,4},{6,5},{7,6},{8,7},{9,8},{10,9... | collective-permute-start | bytes 417800 | tf_op jit(solution)/shard_map/ppermute | solution.py:427
  8.5 0.4 %tables.1 = (f32[504,128]{1,0:T(8,128)S(1)}, bf16[128,512]{1,0:T(8,128)(2,1)S(1)}, bf16[128,512]{1,0:T(8,128)(2,1)S(1)}) custom-call(s32[3,512]{1,0:T(4,128)S(1)} %copy-done.4, f32[3,512]{1,0:T(4,128)S(1)} %copy-done.5, f32[168,128]{1,0:T(8,128)S(1)} %get-tuple-element.17.lanes, f32[8,128]{1,0:T(8,128)S(1)} %get-tuple-element.18.marks), custom_call_target="tpu_custom_call" | custom-call | flops 1073741824 | bytes 8388608 | tf_op jit(solution)/shard_map/tables/pallas_call | solution.py:413
  8.9 1.1 %collective-permute-done.below = f32[272,128]{1,0:T(8,128)S(1)} collective-permute-done((f32[272,128]{1,0:T(8,128)S(1)}, f32[272,128]{1,0:T(8,128)S(1)}, u32[]{:S(2)}, u32[]{:S(2)}) %collective-permute-start) | collective-permute-done | bytes 139296 | tf_op jit(solution)/shard_map/ppermute | solution.py:427
  9.9 6.1 %collective-permute-done.1.above = f32[272,128]{1,0:T(8,128)S(1)} collective-permute-done((f32[272,128]{1,0:T(8,128)S(1)}, f32[272,128]{1,0:T(8,128)S(1)}, u32[]{:S(2)}, u32[]{:S(2)}) %collective-permute-start.1) | collective-permute-done | bytes 139296 | tf_op jit(solution)/shard_map/ppermute | solution.py:427
  16.0 0.2 merge.1
  16.3 0.0 collective-permute-start.2
  16.3 13.7 %collective-permute-start.3 = (f32[160,128]{1,0:T(8,128)S(1)}, f32[160,128]{1,0:T(8,128)S(1)}, u32[]{:S(2)}, u32[]{:S(2)}) collective-permute-start(f32[160,128]{1,0:T(8,128)S(1)} %get-tuple-element.26), channel_id=1, source_target_pairs={{0,960},{64,0},{128,64},{192,128},{256,192},{320,256},{384,320},{4... | collective-permute-start | bytes 245768 | tf_op jit(solution)/shard_map/ppermute | solution.py:427
  29.9 2.1 %collective-permute-done.2.west = f32[160,128]{1,0:T(8,128)S(1)} collective-permute-done((f32[160,128]{1,0:T(8,128)S(1)}, f32[160,128]{1,0:T(8,128)S(1)}, u32[]{:S(2)}, u32[]{:S(2)}) %collective-permute-start.2) | collective-permute-done | bytes 81952 | tf_op jit(solution)/shard_map/ppermute | solution.py:427
  32.0 0.0 collective-permute-done.3.east
  32.0 1.6 %collide.1 = (f32[1216,128]{1,0:T(8,128)}, f32[3,512]{1,0:T(4,128)}) custom-call(f32[1216,128]{1,0:T(8,128)S(1)} %bitcast.4, f32[504,128]{1,0:T(8,128)S(1)} %get-tuple-element.24.force_in, f32[256,128]{1,0:T(8,128)S(1)} %get-tuple-element.20.moment, f32[272,128]{1,0:T(8,128)S(1)} %collective-permute-done.below, f32[272,128]{1,0:T(8,128)S(1)} %collective-permute-done.1.above, ...), custom_call_target="tpu_custom_call" | custom-call | tf_op jit(solution)/shard_map/collide/pallas_call | solution.py:413
  (1 shorter events, 0.0 us)
Async XLA Ops:
  0.6 0.7 %copy-start.1 = (f32[3,1536]{1,0:T(4,128)S(1)}, f32[3,1536]{1,0:T(4,128)}, u32[]{:S(2)}) copy-start(f32[3,1536]{1,0:T(4,128)} %rest.1) | copy-start | bytes 55300
  0.6 1.1 %copy-start = (f32[19,16,4,128]{3,2,1,0:T(4,128)S(1)}, f32[19,16,4,128]{3,2,1,0:T(4,128)}, u32[]{:S(2)}) copy-start(f32[19,16,4,128]{3,2,1,0:T(4,128)} %param.6) | copy-start | bytes 1867780
  0.7 1.1 %copy-start.2 = (s32[2,1536]{1,0:T(2,128)S(1)}, s32[2,1536]{1,0:T(2,128)}, u32[]{:S(2)}) copy-start(s32[2,1536]{1,0:T(2,128)} %edges.1) | copy-start | bytes 36868
  0.7 1.1 %copy-start.3 = (f32[1536]{0:T(1024)S(1)}, f32[1536]{0:T(1024)}, u32[]{:S(2)}) copy-start(f32[1536]{0:T(1024)} %param.10) | copy-start | bytes 18436
  0.7 1.1 %copy-start.4 = (s32[3,512]{1,0:T(4,128)S(1)}, s32[3,512]{1,0:T(4,128)}, u32[]{:S(2)}) copy-start(s32[3,512]{1,0:T(4,128)} %base.3) | copy-start | bytes 18436
  0.7 1.1 %copy-start.5 = (f32[3,512]{1,0:T(4,128)S(1)}, f32[3,512]{1,0:T(4,128)}, u32[]{:S(2)}) copy-start(f32[3,512]{1,0:T(4,128)} %frac.3) | copy-start | bytes 18436
  2.6 7.3 %collective-permute-start = (f32[272,128]{1,0:T(8,128)S(1)}, f32[272,128]{1,0:T(8,128)S(1)}, u32[]{:S(2)}, u32[]{:S(2)}) collective-permute-start(f32[272,128]{1,0:T(8,128)S(1)} %get-tuple-element.22), channel_id=1, source_target_pairs={{0,1},{1,2},{2,3},{3,4},{4,5},{5,6},{6,7},{7,8},{8,9},{9,10},{10,1... | collective-permute-start | bytes 417800 | tf_op jit(solution)/shard_map/ppermute | solution.py:427
  5.7 10.3 %collective-permute-start.1 = (f32[272,128]{1,0:T(8,128)S(1)}, f32[272,128]{1,0:T(8,128)S(1)}, u32[]{:S(2)}, u32[]{:S(2)}) collective-permute-start(f32[272,128]{1,0:T(8,128)S(1)} %get-tuple-element.23), channel_id=1, source_target_pairs={{0,63},{1,0},{2,1},{3,2},{4,3},{5,4},{6,5},{7,6},{8,7},{9,8},{10,9... | collective-permute-start | bytes 417800 | tf_op jit(solution)/shard_map/ppermute | solution.py:427
  16.3 15.8 %collective-permute-start.2 = (f32[160,128]{1,0:T(8,128)S(1)}, f32[160,128]{1,0:T(8,128)S(1)}, u32[]{:S(2)}, u32[]{:S(2)}) collective-permute-start(f32[160,128]{1,0:T(8,128)S(1)} %get-tuple-element.25), channel_id=1, source_target_pairs={{0,64},{64,128},{128,192},{192,256},{256,320},{320,384},{384,448},... | collective-permute-start | bytes 245768 | tf_op jit(solution)/shard_map/ppermute | solution.py:427
  16.3 15.8 %collective-permute-start.3 = (f32[160,128]{1,0:T(8,128)S(1)}, f32[160,128]{1,0:T(8,128)S(1)}, u32[]{:S(2)}, u32[]{:S(2)}) collective-permute-start(f32[160,128]{1,0:T(8,128)S(1)} %get-tuple-element.26), channel_id=1, source_target_pairs={{0,960},{64,0},{128,64},{192,128},{256,192},{320,256},{384,320},{4... | collective-permute-start | bytes 245768 | tf_op jit(solution)/shard_map/ppermute | solution.py:427

commit v4 on v3

--- a/solution.py
+++ b/solution.py
@@ -47,7 +47,10 @@
 POP_ROWS = FORCE_ROWS + 4 * WX
 UP_ROWS = POP_ROWS + 5 * WX
 STRIP_ROWS = UP_ROWS + 4 * WX
-SIDE_ROWS = 3 * 24 + 2 * 32 + 24
+SIDE_MOMENTS = 64
+SIDE_DENSITY = 92
+SIDE_POP = 100
+SIDE_ROWS = 120
 
 
 def outer_weight(r):
@@ -152,22 +155,7 @@
         out[at : at + WX] = pop[pl.ds(q * CELLS + edge_row, WX, stride=WY), :]
 
 
-def spread_kernel(
-    pop,
-    base,
-    frac,
-    edges,
-    stiffness,
-    rest,
-    row,
-    lanes,
-    marks,
-    plane_out,
-    moment,
-    edge_out,
-    up,
-    down,
-):
+def spread_kernel(base, frac, edges, stiffness, rest, row, lanes, marks, plane_out):
     springs = jnp.concatenate([stiffness[k : k + 1] for k in range(EDGES // NZ)], axis=1)
     membrane = edge_forces(base[...], frac[...], edges[...], springs, rest[...], row[...])
     part = frac[...]
@@ -208,6 +196,8 @@
         + along_last(plane_high, load_low)
     )
 
+
+def strips_kernel(pop, lanes, marks, moment, edge_out, up, down):
     density = pop[0:CELLS]
     moments = [None, None, None]
     for q in range(1, 19):
@@ -248,19 +238,28 @@
     low_out[...] = z_low
 
 
-def outgoing(out, force, moment, edge, below, above, sources, spots, offset, dirs):
-    at = 0
-    for x in sources:
-        out[at : at + 21] = force[pl.ds(x, 21, stride=SX), :]
-        at += 24
-    for x in spots:
-        out[at : at + 4] = below[pl.ds(FORCE_ROWS + x, 4, stride=WX), :]
-        for y in range(4):
-            out[at + 4 + y * 4 : at + 8 + y * 4] = moment[pl.ds(x * 4 + y, 4, stride=CELLS), :]
-        out[at + 20 : at + 24] = above[pl.ds(FORCE_ROWS + x, 4, stride=WX), :]
-        out[at + 24 : at + 28] = above[pl.ds(UP_ROWS + x, 4, stride=WX), :]
-        at += 32
-    x = spots[0]
+def outgoing(out, force, moment, edge, below, above, sources, x, behind, offset, dirs):
+    def moments_at(x, y, first):
+        count = 4 - first
+        if y < 0:
+            return below[pl.ds(FORCE_ROWS + first * WX + x, count, stride=WX), :]
+        if y < 4:
+            return moment[pl.ds(first * CELLS + x * 4 + y, count, stride=CELLS), :]
+        at = FORCE_ROWS if y == 4 else UP_ROWS
+        return above[pl.ds(at + first * WX + x, count, stride=WX), :]
+
+    for n, source in enumerate(sources):
+        if source == behind:
+            for y in range(SY):
+                value = force[pl.ds(y * 3 * SX + source, 3, stride=SX), :]
+                value = value + 2.0 * moments_at(source, y - 1, 1)
+                out[21 * n + 3 * y : 21 * n + 3 * y + 3] = value
+                out[SIDE_DENSITY + y : SIDE_DENSITY + y + 1] = moments_at(source, y - 1, 0)[0:1]
+        else:
+            out[21 * n : 21 * n + 21] = force[pl.ds(source, 21, stride=SX), :]
+    for y in range(SY):
+        out[SIDE_MOMENTS + 4 * y : SIDE_MOMENTS + 4 * y + 4] = moments_at(x, y - 1, 0)
+    at = SIDE_POP
     for k, q in enumerate(dirs):
         row = offset + k * 4
         step = lattice_speeds[q][1]
@@ -290,8 +289,8 @@
             for n, x in enumerate((16, 17, 23)):
                 rows = pl.ds((slab * 3 + c) * SX + x, 3, stride=3 * SX)
                 force[rows, :] = force[rows, :] + part[48 + 3 * n : 51 + 3 * n]
-    outgoing(right, force, moment, edge, below, above, (15, 16, 17), (15,), 0, UP_X)
-    outgoing(left, force, moment, edge, below, above, (23, 0, 1), (0, 1), 24, DOWN_X)
+    outgoing(right, force, moment, edge, below, above, (15, 16, 17), 15, None, 0, UP_X)
+    outgoing(left, force, moment, edge, below, above, (23, 0, 1), 0, 1, 24, DOWN_X)
 
 
 def collide_kernel(
@@ -300,10 +299,10 @@
     force[...] = force_in[...]
     for n, x in enumerate((23, 0, 1)):
         rows = pl.ds(x, 21, stride=SX)
-        force[rows, :] = force[rows, :] + west[24 * n : 24 * n + 21]
+        force[rows, :] = force[rows, :] + west[21 * n : 21 * n + 21]
     for n, x in enumerate((15, 16, 17)):
         rows = pl.ds(x, 21, stride=SX)
-        force[rows, :] = force[rows, :] + east[24 * n : 24 * n + 21]
+        force[rows, :] = force[rows, :] + east[21 * n : 21 * n + 21]
 
     for slab in range(SY):
         for q in range(4):
@@ -317,10 +316,10 @@
             else:
                 value = above[UP_ROWS + q * WX : UP_ROWS + (q + 1) * WX]
             ext[row : row + WX] = value
-            ext[row + WX : row + SX] = jnp.ones((8, NZ), f32)
-    ext[pl.ds(23, 28, stride=SX), :] = west[72 : 72 + 28]
-    ext[pl.ds(16, 28, stride=SX), :] = east[72 : 72 + 28]
-    ext[pl.ds(17, 28, stride=SX), :] = east[104 : 104 + 28]
+            ext[row + WX : row + SX] = jnp.full((8, NZ), 0.0 if q else 1.0, f32)
+    ext[pl.ds(23, 28, stride=SX), :] = west[SIDE_MOMENTS : SIDE_MOMENTS + 28]
+    ext[pl.ds(16, 28, stride=SX), :] = east[SIDE_MOMENTS : SIDE_MOMENTS + 28]
+    ext[pl.ds(17, 7, stride=4 * SX), :] = east[SIDE_DENSITY : SIDE_DENSITY + 7]
 
     rate = 1.0 / relax_time
     gain = 1.0 - 0.5 / relax_time
@@ -360,12 +359,12 @@
                 source = POP_ROWS + DOWN_Y.index(q) * WX
                 value = above[source : source + WX]
             if step_x == 1:
-                row = 104 + UP_X.index(q) * 4 + y_to
+                row = SIDE_POP + UP_X.index(q) * 4 + y_to
                 value = jnp.concatenate(
                     [value, jnp.broadcast_to(west[row : row + 1], (8, NZ))], axis=0
                 )
             elif step_x == -1:
-                row = 136 + DOWN_X.index(q) * 4 + y_to
+                row = SIDE_POP + DOWN_X.index(q) * 4 + y_to
                 value = jnp.concatenate(
                     [value, jnp.broadcast_to(east[row : row + 1], (8, NZ))], axis=0
                 )
@@ -431,20 +430,19 @@
     pop = populations.reshape(19 * CELLS, NZ)
     cost = pl.CostEstimate(flops=1 << 30, bytes_accessed=1 << 23, transcendentals=0)
     (row,) = call(rows_kernel, [((TILE, NZ), jnp.int32)], [], "rows", [], cost)
-    lanes, marks, plane, moment, edge, up, down = call(
+    lanes, marks, plane = call(
         spread_kernel,
-        [
-            ((SY * SX, NZ), f32),
-            ((8, NZ), f32),
-            ((SY * SX, VERTS), f32),
-            ((4 * CELLS, NZ), f32),
-            ((48, NZ), f32),
-            ((STRIP_ROWS, NZ), f32),
-            ((STRIP_ROWS, NZ), f32),
-        ],
+        [((SY * SX, NZ), f32), ((8, NZ), f32), ((SY * SX, VERTS), f32)],
         [],
         "spread",
-        [pop, vert_base, vert_frac, edges, stiffness.reshape(EDGES // NZ, NZ), rest, row],
+        [vert_base, vert_frac, edges, stiffness.reshape(EDGES // NZ, NZ), rest, row],
+    )
+    moment, edge, up, down = call(
+        strips_kernel,
+        [((4 * CELLS, NZ), f32), ((48, NZ), f32), ((STRIP_ROWS, NZ), f32), ((STRIP_ROWS, NZ), f32)],
+        [],
+        "strips",
+        [pop, lanes, marks],
     )
     below = shift(up, "gy", 1)
     above = shift(down, "gy", -1)

time: 33.9 us -> 33.4 us (0.985)
    pallas_call x5 -> x6, Pallas kernels: 3.14 us -> 3.18 us  [call(): pl.pallas_call(kernel, out_shape=[jax.ShapeDtypeStruct(shape, kind) for s...]
where the time goes in v4:
time: 33.4 us; the launch traced here: 33.2 us
  starting transfers between devices  19.5 us (58%)
  waiting for transfers between devices  9.02 us (27%)
  Pallas kernels  3.18 us (10%)
  between operations  0.75 us (2%)
  local copies, waits for them, and re-layouts  0.71 us (2%)
    ppermute x4, starting transfers between devices, shift(): lax.ppermute(value, axis, [(i, (i + step) % size) for i in range(size)])  19.5 us
    ppermute x4, waiting for transfers between devices, shift(): lax.ppermute(value, axis, [(i, (i + step) % size) for i in range(size)])  9.02 us
    pallas_call x6, Pallas kernels, call(): pl.pallas_call(kernel, out_shape=[jax.ShapeDtypeStruct(shape, kind) for s...  3.18 us
    unnamed x12, local copies, waits for them, and re-layouts  0.71 us
  transfers between devices with their start and end apart: 4, of which 3 were waited for; matrix products, arithmetic and copies ran while one was open for 0% of the time, Pallas kernels for 1%

profile of v4, /device:TPU:118, one launch (start us, length us, event | category | flops | bytes accessed | tf_op | source)
XLA Modules:
  0.0 33.2 jit_solution(16482440610231860064)
XLA Ops:
  0.6 0.0 copy-start.5
  0.6 0.0 copy-start.4
  0.7 0.0 copy-start.1
  0.7 0.0 copy-start.3
  0.7 0.0 copy-start.2
  0.7 0.0 copy-start
  0.7 0.6 %copy-done.5 = f32[3,512]{1,0:T(4,128)S(1)} copy-done((f32[3,512]{1,0:T(4,128)S(1)}, f32[3,512]{1,0:T(4,128)}, u32[]{:S(2)}) %copy-start.5) | copy-done | bytes 6168
  1.3 0.0 copy-done.4
  1.3 0.1 copy-done.1
  1.4 0.0 copy-done.3
  1.4 0.0 copy-done.2
  1.4 0.9 %spread.1 = (f32[168,128]{1,0:T(8,128)S(1)}, f32[8,128]{1,0:T(8,128)S(1)}, f32[168,512]{1,0:T(8,128)S(1)}) custom-call(s32[3,512]{1,0:T(4,128)S(1)} %copy-done.4, f32[3,512]{1,0:T(4,128)S(1)} %copy-done.5, s32[2,1536]{1,0:T(2,128)S(1)} %copy-done.2, f32[12,128]{1,0:T(8,128)S(1)} %bitcast.5, f32[3,1536]{1,0:T(4,128)S(1)} %copy-done.1, s32[128,128]{1,0:T(8,128)S(1)} %rows.1.row), custom_call_target="tpu_custom_call" | custom-call | tf_op jit(solution)/shard_map/spread/pallas_call | solution.py:412
  2.3 0.0 copy-done
  2.3 0.1 strips.1
  2.4 3.0 %collective-permute-start = (f32[272,128]{1,0:T(8,128)S(1)}, f32[272,128]{1,0:T(8,128)S(1)}, u32[]{:S(2)}, u32[]{:S(2)}) collective-permute-start(f32[272,128]{1,0:T(8,128)S(1)} %get-tuple-element.22), channel_id=1, source_target_pairs={{0,1},{1,2},{2,3},{3,4},{4,5},{5,6},{6,7},{7,8},{8,9},{9,10},{10,1... | collective-permute-start | bytes 417800 | tf_op jit(solution)/shard_map/ppermute | solution.py:426
  5.4 2.8 %collective-permute-start.1 = (f32[272,128]{1,0:T(8,128)S(1)}, f32[272,128]{1,0:T(8,128)S(1)}, u32[]{:S(2)}, u32[]{:S(2)}) collective-permute-start(f32[272,128]{1,0:T(8,128)S(1)} %get-tuple-element.23), channel_id=1, source_target_pairs={{0,63},{1,0},{2,1},{3,2},{4,3},{5,4},{6,5},{7,6},{8,7},{9,8},{10,9... | collective-permute-start | bytes 417800 | tf_op jit(solution)/shard_map/ppermute | solution.py:426
  8.2 0.4 %tables.1 = (f32[504,128]{1,0:T(8,128)S(1)}, bf16[128,512]{1,0:T(8,128)(2,1)S(1)}, bf16[128,512]{1,0:T(8,128)(2,1)S(1)}) custom-call(s32[3,512]{1,0:T(4,128)S(1)} %copy-done.4, f32[3,512]{1,0:T(4,128)S(1)} %copy-done.5, f32[168,128]{1,0:T(8,128)S(1)} %get-tuple-element.17.lanes, f32[8,128]{1,0:T(8,128)S(1)} %get-tuple-element.18.marks), custom_call_target="tpu_custom_call" | custom-call | flops 1073741824 | bytes 8388608 | tf_op jit(solution)/shard_map/tables/pallas_call | solution.py:412
  8.6 1.1 %collective-permute-done.below = f32[272,128]{1,0:T(8,128)S(1)} collective-permute-done((f32[272,128]{1,0:T(8,128)S(1)}, f32[272,128]{1,0:T(8,128)S(1)}, u32[]{:S(2)}, u32[]{:S(2)}) %collective-permute-start) | collective-permute-done | bytes 139296 | tf_op jit(solution)/shard_map/ppermute | solution.py:426
  9.7 6.1 %collective-permute-done.1.above = f32[272,128]{1,0:T(8,128)S(1)} collective-permute-done((f32[272,128]{1,0:T(8,128)S(1)}, f32[272,128]{1,0:T(8,128)S(1)}, u32[]{:S(2)}, u32[]{:S(2)}) %collective-permute-start.1) | collective-permute-done | bytes 139296 | tf_op jit(solution)/shard_map/ppermute | solution.py:426
  15.7 0.3 merge.1
  16.0 0.0 collective-permute-start.2
  16.0 13.7 %collective-permute-start.3 = (f32[120,128]{1,0:T(8,128)S(1)}, f32[120,128]{1,0:T(8,128)S(1)}, u32[]{:S(2)}, u32[]{:S(2)}) collective-permute-start(f32[120,128]{1,0:T(8,128)S(1)} %get-tuple-element.26), channel_id=1, source_target_pairs={{0,960},{64,0},{128,64},{192,128},{256,192},{320,256},{384,320},{4... | collective-permute-start | bytes 184328 | tf_op jit(solution)/shard_map/ppermute | solution.py:426
  29.7 1.9 %collective-permute-done.2.west = f32[120,128]{1,0:T(8,128)S(1)} collective-permute-done((f32[120,128]{1,0:T(8,128)S(1)}, f32[120,128]{1,0:T(8,128)S(1)}, u32[]{:S(2)}, u32[]{:S(2)}) %collective-permute-start.2) | collective-permute-done | bytes 61472 | tf_op jit(solution)/shard_map/ppermute | solution.py:426
  31.6 0.0 collective-permute-done.3.east
  31.6 1.6 %collide.1 = (f32[1216,128]{1,0:T(8,128)}, f32[3,512]{1,0:T(4,128)}) custom-call(f32[1216,128]{1,0:T(8,128)S(1)} %bitcast.4, f32[504,128]{1,0:T(8,128)S(1)} %get-tuple-element.24.force_in, f32[256,128]{1,0:T(8,128)S(1)} %get-tuple-element.20.moment, f32[272,128]{1,0:T(8,128)S(1)} %collective-permute-done.below, f32[272,128]{1,0:T(8,128)S(1)} %collective-permute-done.1.above, ...), custom_call_target="tpu_custom_call" | custom-call | tf_op jit(solution)/shard_map/collide/pallas_call | solution.py:412
  (1 shorter events, 0.0 us)
Async XLA Ops:
  0.6 0.7 %copy-start.5 = (f32[3,512]{1,0:T(4,128)S(1)}, f32[3,512]{1,0:T(4,128)}, u32[]{:S(2)}) copy-start(f32[3,512]{1,0:T(4,128)} %frac.3) | copy-start | bytes 18436
  0.6 0.7 %copy-start.4 = (s32[3,512]{1,0:T(4,128)S(1)}, s32[3,512]{1,0:T(4,128)}, u32[]{:S(2)}) copy-start(s32[3,512]{1,0:T(4,128)} %base.3) | copy-start | bytes 18436
  0.7 0.8 %copy-start.1 = (f32[3,1536]{1,0:T(4,128)S(1)}, f32[3,1536]{1,0:T(4,128)}, u32[]{:S(2)}) copy-start(f32[3,1536]{1,0:T(4,128)} %rest.1) | copy-start | bytes 55300
  0.7 0.7 %copy-start.3 = (f32[1536]{0:T(1024)S(1)}, f32[1536]{0:T(1024)}, u32[]{:S(2)}) copy-start(f32[1536]{0:T(1024)} %param.10) | copy-start | bytes 18436
  0.7 0.7 %copy-start.2 = (s32[2,1536]{1,0:T(2,128)S(1)}, s32[2,1536]{1,0:T(2,128)}, u32[]{:S(2)}) copy-start(s32[2,1536]{1,0:T(2,128)} %edges.1) | copy-start | bytes 36868
  0.7 1.6 %copy-start = (f32[19,16,4,128]{3,2,1,0:T(4,128)S(1)}, f32[19,16,4,128]{3,2,1,0:T(4,128)}, u32[]{:S(2)}) copy-start(f32[19,16,4,128]{3,2,1,0:T(4,128)} %param.6) | copy-start | bytes 1867780
  2.4 7.3 %collective-permute-start = (f32[272,128]{1,0:T(8,128)S(1)}, f32[272,128]{1,0:T(8,128)S(1)}, u32[]{:S(2)}, u32[]{:S(2)}) collective-permute-start(f32[272,128]{1,0:T(8,128)S(1)} %get-tuple-element.22), channel_id=1, source_target_pairs={{0,1},{1,2},{2,3},{3,4},{4,5},{5,6},{6,7},{7,8},{8,9},{9,10},{10,1... | collective-permute-start | bytes 417800 | tf_op jit(solution)/shard_map/ppermute | solution.py:426
  5.4 10.3 %collective-permute-start.1 = (f32[272,128]{1,0:T(8,128)S(1)}, f32[272,128]{1,0:T(8,128)S(1)}, u32[]{:S(2)}, u32[]{:S(2)}) collective-permute-start(f32[272,128]{1,0:T(8,128)S(1)} %get-tuple-element.23), channel_id=1, source_target_pairs={{0,63},{1,0},{2,1},{3,2},{4,3},{5,4},{6,5},{7,6},{8,7},{9,8},{10,9... | collective-permute-start | bytes 417800 | tf_op jit(solution)/shard_map/ppermute | solution.py:426
  16.0 15.6 %collective-permute-start.2 = (f32[120,128]{1,0:T(8,128)S(1)}, f32[120,128]{1,0:T(8,128)S(1)}, u32[]{:S(2)}, u32[]{:S(2)}) collective-permute-start(f32[120,128]{1,0:T(8,128)S(1)} %get-tuple-element.25), channel_id=1, source_target_pairs={{0,64},{64,128},{128,192},{192,256},{256,320},{320,384},{384,448},... | collective-permute-start | bytes 184328 | tf_op jit(solution)/shard_map/ppermute | solution.py:426
  16.0 15.6 %collective-permute-start.3 = (f32[120,128]{1,0:T(8,128)S(1)}, f32[120,128]{1,0:T(8,128)S(1)}, u32[]{:S(2)}, u32[]{:S(2)}) collective-permute-start(f32[120,128]{1,0:T(8,128)S(1)} %get-tuple-element.26), channel_id=1, source_target_pairs={{0,960},{64,0},{128,64},{192,128},{256,192},{320,256},{384,320},{4... | collective-permute-start | bytes 184328 | tf_op jit(solution)/shard_map/ppermute | solution.py:426

commit v5 on v4

--- a/solution.py
+++ b/solution.py
@@ -51,6 +51,8 @@
 SIDE_DENSITY = 92
 SIDE_POP = 100
 SIDE_ROWS = 120
+INNER = 13
+RIM = (23, 0, 1, 15, 16, 17)
 
 
 def outer_weight(r):
@@ -155,7 +157,7 @@
         out[at : at + WX] = pop[pl.ds(q * CELLS + edge_row, WX, stride=WY), :]
 
 
-def spread_kernel(base, frac, edges, stiffness, rest, row, lanes, marks, plane_out):
+def spread_kernel(base, frac, edges, stiffness, rest, row, lanes, marks, inner_out, rim_out):
     springs = jnp.concatenate([stiffness[k : k + 1] for k in range(EDGES // NZ)], axis=1)
     membrane = edge_forces(base[...], frac[...], edges[...], springs, rest[...], row[...])
     part = frac[...]
@@ -168,7 +170,9 @@
     slab = iota((8, VERTS), 0)
     along_y = columns([k[1:2] for k in kernel], slab - (cell[1:2] & (WY - 1)))
     plane = jnp.concatenate([along_x * along_y[y : y + 1] for y in range(SY)], axis=0)
-    plane_out[...] = plane
+    inside = jnp.where(iota((WX, VERTS), 0) < INNER, along_x[2 : 2 + WX], 0.0)
+    inner_out[...] = jnp.concatenate([inside * along_y[y : y + 1] for y in range(SY)], axis=0)
+    rim_out[...] = jnp.concatenate([along_x[x : x + 1] * along_y for x in RIM], axis=0)
 
     layer = iota((8, TILE), 0)
     lane = iota((1, TILE), 1)
@@ -293,119 +297,194 @@
     outgoing(left, force, moment, edge, below, above, (23, 0, 1), 0, 1, 24, DOWN_X)
 
 
-def collide_kernel(
-    pop, force_in, moment, below, above, west, east, plane, z_high, z_low, fresh, sampled, force, ext, speed
-):
-    force[...] = force_in[...]
-    for n, x in enumerate((23, 0, 1)):
-        rows = pl.ds(x, 21, stride=SX)
-        force[rows, :] = force[rows, :] + west[21 * n : 21 * n + 21]
-    for n, x in enumerate((15, 16, 17)):
-        rows = pl.ds(x, 21, stride=SX)
-        force[rows, :] = force[rows, :] + east[21 * n : 21 * n + 21]
-
-    for slab in range(SY):
-        for q in range(4):
-            row = (slab * 4 + q) * SX
-            if slab == 0:
-                value = below[FORCE_ROWS + q * WX : FORCE_ROWS + (q + 1) * WX]
-            elif slab < 5:
-                value = moment[pl.ds(q * CELLS + slab - 1, WX, stride=WY), :]
-            elif slab == 5:
-                value = above[FORCE_ROWS + q * WX : FORCE_ROWS + (q + 1) * WX]
-            else:
-                value = above[UP_ROWS + q * WX : UP_ROWS + (q + 1) * WX]
-            ext[row : row + WX] = value
-            ext[row + WX : row + SX] = jnp.full((8, NZ), 0.0 if q else 1.0, f32)
-    ext[pl.ds(23, 28, stride=SX), :] = west[SIDE_MOMENTS : SIDE_MOMENTS + 28]
-    ext[pl.ds(16, 28, stride=SX), :] = east[SIDE_MOMENTS : SIDE_MOMENTS + 28]
-    ext[pl.ds(17, 7, stride=4 * SX), :] = east[SIDE_DENSITY : SIDE_DENSITY + 7]
-
+def collide(density, momentum, pull):
     rate = 1.0 / relax_time
     gain = 1.0 - 0.5 / relax_time
+    inverse = 1.0 / density
+    flow = [(momentum[c] + 0.5 * pull[c]) * inverse for c in range(3)]
+    square = flow[0] * flow[0] + flow[1] * flow[1] + flow[2] * flow[2]
+    work = flow[0] * pull[0] + flow[1] * pull[1] + flow[2] * pull[2]
+    scaled = rate * density
+    constant = scaled * (1.0 - 1.5 * square) - (3.0 * gain) * work
+    linear = 3.0 * scaled
+    quadratic = 4.5 * scaled
+
+    def directed(vectors, q):
+        total = None
+        for c in range(3):
+            s = lattice_speeds[q][c]
+            if s:
+                if total is None:
+                    total = vectors[c] if s > 0 else -vectors[c]
+                else:
+                    total = total + vectors[c] if s > 0 else total - vectors[c]
+        return total
+
+    def gained(q):
+        if q == 0:
+            return lattice_weights[0] * constant
+        cu = directed(flow, q)
+        cf = directed(pull, q)
+        balance = constant + cu * (linear + quadratic * cu + (9.0 * gain) * cf) + (3.0 * gain) * cf
+        return lattice_weights[q] * balance
+
+    return flow, gained
+
+
+def moved_z(post, q):
+    step = lattice_speeds[q][2]
+    return pltpu.roll(post, step % NZ, 1) if step else post
+
+
+def sample(speeds, plane, z_high, z_low):
+    high, low = halves(speeds)
+    split = jnp.concatenate([high.astype(f32), low.astype(f32)], axis=1).astype(bf16)
+    both = jnp.concatenate([z_high, z_high], axis=0)
+    value = jnp.dot(split, both, preferred_element_type=f32)
+    value = value + jnp.dot(high, z_low, preferred_element_type=f32)
+    return jnp.sum(value * plane, axis=0, keepdims=True)
+
+
+def inner_kernel(pop, force, moment, below, above, plane, z_high, z_low, fresh, kept, sampled, speed):
+    left = 1.0 - 1.0 / relax_time
     for slab in range(SY):
-        density = ext[slab * 4 * SX : (slab * 4 + 1) * SX]
-        inverse = 1.0 / density
-        pull = [force[(slab * 3 + c) * SX : (slab * 3 + c + 1) * SX] for c in range(3)]
-        flow = [
-            (ext[(slab * 4 + 1 + c) * SX : (slab * 4 + 2 + c) * SX] + 0.5 * pull[c]) * inverse
-            for c in range(3)
-        ]
+        y_from = slab - 1
+        known = []
+        for q in range(4):
+            if slab == 0:
+                at = FORCE_ROWS + q * WX + 2
+                known.append(below[at : at + INNER])
+            elif slab < 5:
+                known.append(moment[pl.ds(q * CELLS + 2 * WY + y_from, INNER, stride=WY), :])
+            else:
+                at = (FORCE_ROWS if slab == 5 else UP_ROWS) + q * WX + 2
+                known.append(above[at : at + INNER])
+        pull = []
         for c in range(3):
-            high, low = halves(flow[c])
-            row = (c * SY + slab) * SX
-            speed[row : row + SX, 0:NZ] = high.astype(f32)
-            speed[row : row + SX, NZ : 2 * NZ] = low.astype(f32)
-        if slab == SY - 1:
-            continue
-        y_from = slab - 1
-        square = flow[0] * flow[0] + flow[1] * flow[1] + flow[2] * flow[2]
-        work = flow[0] * pull[0] + flow[1] * pull[1] + flow[2] * pull[2]
-        scaled = rate * density
-        constant = scaled * (1.0 - 1.5 * square) - (3.0 * gain) * work
-        linear = 3.0 * scaled
-        quadratic = 4.5 * scaled
+            row = (slab * 3 + c) * SX + 2
+            pull.append(force[row : row + INNER])
+        flow, gained = collide(known[0], known[1:], pull)
+        for c in range(3):
+            row = (c * SY + slab) * WX
+            speed[row : row + WX] = jnp.concatenate([flow[c], jnp.zeros((3, NZ), f32)], axis=0)
         for q in range(19):
-            step_x, step_y, step_z = lattice_speeds[q]
+            step_x, step_y, _ = lattice_speeds[q]
             y_to = y_from + step_y
-            if y_to < 0 or y_to > 3:
+            if y_from == 5 or y_to < 0 or y_to > 3:
                 continue
             if 0 <= y_from <= 3:
-                value = pop[pl.ds(q * CELLS + y_from, WX, stride=WY), :]
+                value = pop[pl.ds(q * CELLS + 2 * WY + y_from, INNER, stride=WY), :]
             elif y_from < 0:
-                source = POP_ROWS + UP_Y.index(q) * WX
-                value = below[source : source + WX]
+                at = POP_ROWS + UP_Y.index(q) * WX + 2
+                value = below[at : at + INNER]
             else:
-                source = POP_ROWS + DOWN_Y.index(q) * WX
-                value = above[source : source + WX]
-            if step_x == 1:
-                row = SIDE_POP + UP_X.index(q) * 4 + y_to
-                value = jnp.concatenate(
-                    [value, jnp.broadcast_to(west[row : row + 1], (8, NZ))], axis=0
-                )
-            elif step_x == -1:
-                row = SIDE_POP + DOWN_X.index(q) * 4 + y_to
-                value = jnp.concatenate(
-                    [value, jnp.broadcast_to(east[row : row + 1], (8, NZ))], axis=0
-                )
-            extent = value.shape[0]
-
-            def directed(vectors):
-                total = None
-                for c in range(3):
-                    s = lattice_speeds[q][c]
-                    if s:
-                        term = vectors[c][0:extent]
-                        if total is None:
-                            total = term if s > 0 else -term
-                        else:
-                            total = total + term if s > 0 else total - term
-                return total
-
-            balance = constant[0:extent]
-            if q:
-                cu = directed(flow)
-                cf = directed(pull)
-                balance = (
-                    balance
-                    + cu * (linear[0:extent] + quadratic[0:extent] * cu + (9.0 * gain) * cf)
-                    + (3.0 * gain) * cf
-                )
-            post = (1.0 - rate) * value + lattice_weights[q] * balance
-            if step_x:
-                post = pltpu.roll(post, step_x % SX, 0)[0:WX]
-            if step_z:
-                post = pltpu.roll(post, step_z % NZ, 1)
-            fresh[pl.ds(q * CELLS + y_to, WX, stride=WY), :] = post
-
-    both = jnp.concatenate([z_high[...], z_high[...]], axis=0)
-    rows = SY * SX
+                at = POP_ROWS + DOWN_Y.index(q) * WX + 2
+                value = above[at : at + INNER]
+            post = moved_z(left * value + gained(q), q)
+            fresh[pl.ds(q * CELLS + (2 + step_x) * WY + y_to, INNER, stride=WY), :] = post
+    for q in range(19):
+        for n, x in enumerate(KEPT[lattice_speeds[q][0]]):
+            at = q * CELLS + x * WY
+            kept[q, n] = fresh[at : at + WY]
+    rows = SY * WX
     for c in range(3):
-        split = speed[c * rows : (c + 1) * rows].astype(bf16)
-        value = jnp.dot(split, both, preferred_element_type=f32) + jnp.dot(
-            split[:, 0:NZ], z_low[...], preferred_element_type=f32
-        )
-        sampled[c : c + 1] = jnp.sum(value * plane[...], axis=0, keepdims=True)
+        sampled[c : c + 1] = sample(speed[c * rows : (c + 1) * rows], plane[...], z_high[...], z_low[...])
+
+
+KEPT = {0: (2, 14), 1: (14, 15), -1: (1, 2)}
+
+
+def rim_kernel(
+    fresh_in,
+    kept,
+    part,
+    pop,
+    force,
+    moment,
+    below,
+    above,
+    west,
+    east,
+    plane,
+    z_high,
+    z_low,
+    fresh,
+    sampled_far,
+    low_side,
+    high_side,
+    sampled,
+    sent,
+):
+    left = 1.0 - 1.0 / relax_time
+    speeds = [[], [], []]
+    for n, slot in enumerate(RIM):
+        x = -1 if slot == 23 else slot
+        side = west if n < 3 else east
+        pull = []
+        for c in range(3):
+            value = force[pl.ds(c * SX + slot, SY, stride=3 * SX), :]
+            value = value + side[pl.ds(21 * (n % 3) + c, SY, stride=3), :]
+            pull.append(jnp.concatenate([value, jnp.zeros((1, NZ), f32)], axis=0))
+        known = []
+        for q in range(4):
+            fill = jnp.full((1, NZ), 0.0 if q else 1.0, f32)
+            if x in (-1, 16):
+                rows = [side[pl.ds(SIDE_MOMENTS + q, SY, stride=4), :], fill]
+            elif x == 17:
+                if q:
+                    rows = [jnp.zeros((8, NZ), f32)]
+                else:
+                    rows = [side[SIDE_DENSITY : SIDE_DENSITY + SY], fill]
+            else:
+                near, far = FORCE_ROWS + q * WX + x, UP_ROWS + q * WX + x
+                own = q * CELLS + x * WY
+                rows = [below[near : near + 1], moment[own : own + WY], above[near : near + 1], above[far : far + 1], fill]
+            known.append(jnp.concatenate(rows, axis=0) if len(rows) > 1 else rows[0])
+        flow, gained = collide(known[0], known[1:], pull)
+        for c in range(3):
+            speeds[c].append(flow[c])
+        for q in range(19):
+            step_x, step_y, _ = lattice_speeds[q]
+            x_to = x + step_x
+            if x_to not in (0, 1, 2, 14, 15) or (x == 15 and step_x == 1) or x == 17:
+                continue
+            own = q * CELLS + x * WY
+            if x in (-1, 16):
+                at = SIDE_POP + (UP_X if x < 0 else DOWN_X).index(q) * 4
+                value = side[at : at + 4]
+            elif step_y == 0:
+                value = pop[own : own + 4]
+            elif step_y == 1:
+                at = POP_ROWS + UP_Y.index(q) * WX + x
+                value = jnp.concatenate([below[at : at + 1], pop[own : own + 3]], axis=0)
+            else:
+                at = POP_ROWS + DOWN_Y.index(q) * WX + x
+                value = jnp.concatenate([pop[own + 1 : own + 4], above[at : at + 1]], axis=0)
+            post = moved_z(left * value + gained(q)[1 - step_y : 5 - step_y], q)
+            if x_to < 3:
+                low_side[q, x_to] = post
+            else:
+                high_side[q, x_to - 14] = post
+    for q in range(19):
+        for n, x in enumerate(KEPT[lattice_speeds[q][0]]):
+            if x < 3:
+                low_side[q, x] = kept[q, n]
+            else:
+                high_side[q, x - 14] = kept[q, n]
+    copies = [
+        pltpu.make_async_copy(low_side, fresh.at[:, 0:3], sent.at[0]),
+        pltpu.make_async_copy(high_side, fresh.at[:, 14:16], sent.at[1]),
+    ]
+    for copy in copies:
+        copy.start()
+    for c in range(3):
+        total = sample(jnp.concatenate(speeds[c], axis=0), plane[...], z_high[...], z_low[...])
+        sampled[c : c + 1] = part[c : c + 1] + total
+    last = pltpu.make_async_copy(sampled, sampled_far, sent.at[2])
+    last.start()
+    for copy in copies:
+        copy.wait()
+    last.wait()
 
 
 def call(kernel, outputs, scratch, name, operands, cost=None):
@@ -430,9 +509,9 @@
     pop = populations.reshape(19 * CELLS, NZ)
     cost = pl.CostEstimate(flops=1 << 30, bytes_accessed=1 << 23, transcendentals=0)
     (row,) = call(rows_kernel, [((TILE, NZ), jnp.int32)], [], "rows", [], cost)
-    lanes, marks, plane = call(
+    lanes, marks, inner_plane, rim_plane = call(
         spread_kernel,
-        [((SY * SX, NZ), f32), ((8, NZ), f32), ((SY * SX, VERTS), f32)],
+        [((SY * SX, NZ), f32), ((8, NZ), f32), ((SY * WX, VERTS), f32), ((48, VERTS), f32)],
         [],
         "spread",
         [vert_base, vert_frac, edges, stiffness.reshape(EDGES // NZ, NZ), rest, row],
@@ -463,18 +542,48 @@
     )
     west = shift(right, "gx", 1)
     east = shift(left, "gx", -1)
-    fresh, sampled = call(
-        collide_kernel,
-        [((19 * CELLS, NZ), f32), ((3, VERTS), f32)],
-        [
-            pltpu.VMEM((SY * 3 * SX, NZ), f32),
-            pltpu.VMEM((SY * 4 * SX, NZ), f32),
-            pltpu.VMEM((SY * 3 * SX, 2 * NZ), f32),
+    fresh, kept, part = call(
+        inner_kernel,
+        [((19 * CELLS, NZ), f32), ((19, 2, WY, NZ), f32), ((3, VERTS), f32)],
+        [pltpu.VMEM((3 * SY * WX, NZ), f32)],
+        "inner",
+        [pop, force, moment, below, above, inner_plane, z_high, z_low],
+        cost,
+    )
+    vmem = pl.BlockSpec(memory_space=pltpu.VMEM)
+    far = pl.BlockSpec(memory_space=pltpu.HBM)
+    return pl.pallas_call(
+        rim_kernel,
+        out_shape=[
+            jax.ShapeDtypeStruct((19, WX, WY, NZ), f32),
+            jax.ShapeDtypeStruct((3, VERTS), f32),
         ],
-        "collide",
-        [pop, force, moment, below, above, west, east, plane, z_high, z_low],
-    )
-    return fresh.reshape(19, WX, WY, NZ), sampled
+        in_specs=[far] + [vmem] * 12,
+        out_specs=[far, far],
+        scratch_shapes=[
+            pltpu.VMEM((19, 3, WY, NZ), f32),
+            pltpu.VMEM((19, 2, WY, NZ), f32),
+            pltpu.VMEM((3, VERTS), f32),
+            pltpu.SemaphoreType.DMA((3,)),
+        ],
+        input_output_aliases={0: 0},
+        compiler_params=pltpu.CompilerParams(vmem_limit_bytes=32 * 1024 * 1024),
+        name="rim",
+    )(
+        fresh.reshape(19, WX, WY, NZ),
+        kept,
+        part,
+        pop,
+        force,
+        moment,
+        below,
+        above,
+        west,
+        east,
+        rim_plane,
+        z_high,
+        z_low,
+    )
 
 
 def solution(mesh):

time: 33.4 us -> 32.8 us (0.982)
  waiting for transfers between devices: 9.02 us -> 7.65 us
  Pallas kernels: 3.18 us -> 3.95 us
    ppermute x4, waiting for transfers between devices: 9.02 us -> 7.65 us  [shift(): lax.ppermute(value, axis, [(i, (i + step) % size) for i in range(size)])]
    pallas_call x0 -> x1, Pallas kernels: none -> 1.01 us  [per_device(): pl.pallas_call(rim_kernel, out_shape=[jax.ShapeDtypeStruct((19, WX, WY, N...]
  transfers between devices with their start and end apart: 4 -> 4, of which waited for: 3 -> 3; matrix products, arithmetic and copies ran while one was open for 0% -> 0% of each run, Pallas kernels for 1% -> 5%
where the time goes in v5:
time: 32.8 us; the launch traced here: 32.6 us
  starting transfers between devices  19.5 us (59%)
  waiting for transfers between devices  7.65 us (23%)
  Pallas kernels  3.95 us (12%)
  between operations  0.75 us (2%)
  local copies, waits for them, and re-layouts  0.71 us (2%)
    ppermute x4, starting transfers between devices, shift(): lax.ppermute(value, axis, [(i, (i + step) % size) for i in range(size)])  19.5 us
    ppermute x4, waiting for transfers between devices, shift(): lax.ppermute(value, axis, [(i, (i + step) % size) for i in range(size)])  7.65 us
    pallas_call x6, Pallas kernels, call(): pl.pallas_call(kernel, out_shape=[jax.ShapeDtypeStruct(shape, kind) for s...  2.95 us
    pallas_call x1, Pallas kernels, per_device(): pl.pallas_call(rim_kernel, out_shape=[jax.ShapeDtypeStruct((19, WX, WY, N...  1.01 us
    unnamed x12, local copies, waits for them, and re-layouts  0.71 us
  transfers between devices with their start and end apart: 4, of which 3 were waited for; matrix products, arithmetic and copies ran while one was open for 0% of the time, Pallas kernels for 5%

profile of v5, /device:TPU:118, one launch (start us, length us, event | category | flops | bytes accessed | tf_op | source)
XLA Modules:
  0.0 32.6 jit_solution(12010832470989540694)
XLA Ops:
  0.6 0.0 copy-start.5
  0.6 0.0 copy-start.4
  0.7 0.0 copy-start.1
  0.7 0.0 copy-start.3
  0.7 0.0 copy-start.2
  0.7 0.0 copy-start
  0.7 0.6 %copy-done.5 = f32[3,512]{1,0:T(4,128)S(1)} copy-done((f32[3,512]{1,0:T(4,128)S(1)}, f32[3,512]{1,0:T(4,128)}, u32[]{:S(2)}) %copy-start.5) | copy-done | bytes 6168
  1.3 0.0 copy-done.4
  1.3 0.1 copy-done.1
  1.4 0.0 copy-done.3
  1.4 0.0 copy-done.2
  1.4 0.9 %spread.1 = (f32[168,128]{1,0:T(8,128)S(1)}, f32[8,128]{1,0:T(8,128)S(1)}, f32[112,512]{1,0:T(8,128)S(1)}, f32[48,512]{1,0:T(8,128)S(1)}) custom-call(s32[3,512]{1,0:T(4,128)S(1)} %copy-done.4, f32[3,512]{1,0:T(4,128)S(1)} %copy-done.5, s32[2,1536]{1,0:T(2,128)S(1)} %copy-done.2, f32[12,128]{1,0:T(8,128)S(1)} %bitcast.6, f32[3,1536]{1,0:T(4,128)S(1)} %copy-done.1, ...), custom_call_target="tpu_custom_call" | custom-call | tf_op jit(solution)/shard_map/spread/pallas_call | solution.py:491
  2.3 0.0 copy-done
  2.3 0.1 strips.1
  2.4 3.0 %collective-permute-start = (f32[272,128]{1,0:T(8,128)S(1)}, f32[272,128]{1,0:T(8,128)S(1)}, u32[]{:S(2)}, u32[]{:S(2)}) collective-permute-start(f32[272,128]{1,0:T(8,128)S(1)} %get-tuple-element.24), channel_id=1, source_target_pairs={{0,1},{1,2},{2,3},{3,4},{4,5},{5,6},{6,7},{7,8},{8,9},{9,10},{10,1... | collective-permute-start | bytes 417800 | tf_op jit(solution)/shard_map/ppermute | solution.py:505
  5.4 2.8 %collective-permute-start.1 = (f32[272,128]{1,0:T(8,128)S(1)}, f32[272,128]{1,0:T(8,128)S(1)}, u32[]{:S(2)}, u32[]{:S(2)}) collective-permute-start(f32[272,128]{1,0:T(8,128)S(1)} %get-tuple-element.25), channel_id=1, source_target_pairs={{0,63},{1,0},{2,1},{3,2},{4,3},{5,4},{6,5},{7,6},{8,7},{9,8},{10,9... | collective-permute-start | bytes 417800 | tf_op jit(solution)/shard_map/ppermute | solution.py:505
  8.2 0.4 %tables.1 = (f32[504,128]{1,0:T(8,128)S(1)}, bf16[128,512]{1,0:T(8,128)(2,1)S(1)}, bf16[128,512]{1,0:T(8,128)(2,1)S(1)}) custom-call(s32[3,512]{1,0:T(4,128)S(1)} %copy-done.4, f32[3,512]{1,0:T(4,128)S(1)} %copy-done.5, f32[168,128]{1,0:T(8,128)S(1)} %get-tuple-element.19.lanes, f32[8,128]{1,0:T(8,128)S(1)} %get-tuple-element.20.marks), custom_call_target="tpu_custom_call" | custom-call | flops 1073741824 | bytes 8388608 | tf_op jit(solution)/shard_map/tables/pallas_call | solution.py:491
  8.6 1.1 %collective-permute-done.below = f32[272,128]{1,0:T(8,128)S(1)} collective-permute-done((f32[272,128]{1,0:T(8,128)S(1)}, f32[272,128]{1,0:T(8,128)S(1)}, u32[]{:S(2)}, u32[]{:S(2)}) %collective-permute-start) | collective-permute-done | bytes 139296 | tf_op jit(solution)/shard_map/ppermute | solution.py:505
  9.7 6.1 %collective-permute-done.1.above = f32[272,128]{1,0:T(8,128)S(1)} collective-permute-done((f32[272,128]{1,0:T(8,128)S(1)}, f32[272,128]{1,0:T(8,128)S(1)}, u32[]{:S(2)}, u32[]{:S(2)}) %collective-permute-start.1) | collective-permute-done | bytes 139296 | tf_op jit(solution)/shard_map/ppermute | solution.py:505
  15.8 0.3 merge.1
  16.0 0.0 collective-permute-start.2
  16.0 13.7 %collective-permute-start.3 = (f32[120,128]{1,0:T(8,128)S(1)}, f32[120,128]{1,0:T(8,128)S(1)}, u32[]{:S(2)}, u32[]{:S(2)}) collective-permute-start(f32[120,128]{1,0:T(8,128)S(1)} %get-tuple-element.34), channel_id=1, source_target_pairs={{0,960},{64,0},{128,64},{192,128},{256,192},{320,256},{384,320},{4... | collective-permute-start | bytes 184328 | tf_op jit(solution)/shard_map/ppermute | solution.py:505
  29.7 1.4 %inner.1 = (f32[1216,128]{1,0:T(8,128)}, f32[19,2,4,128]{3,2,1,0:T(4,128)S(1)}, f32[3,512]{1,0:T(4,128)S(1)}) custom-call(f32[1216,128]{1,0:T(8,128)S(1)} %bitcast.4, f32[504,128]{1,0:T(8,128)S(1)} %get-tuple-element.26.force, f32[256,128]{1,0:T(8,128)S(1)} %get-tuple-element.22.moment, f32[272,128]{1,0:T(8,128)S(1)} %collective-permute-done.below, ...), custom_call_target="tpu_custom_call" | custom-call | flops 1073741824 | bytes 8388608 | tf_op jit(solution)/shard_map/inner/pallas_call | solution.py:491
  31.1 0.5 %collective-permute-done.2.west = f32[120,128]{1,0:T(8,128)S(1)} collective-permute-done((f32[120,128]{1,0:T(8,128)S(1)}, f32[120,128]{1,0:T(8,128)S(1)}, u32[]{:S(2)}, u32[]{:S(2)}) %collective-permute-start.2) | collective-permute-done | bytes 61472 | tf_op jit(solution)/shard_map/ppermute | solution.py:505
  31.6 0.0 collective-permute-done.3.east
  31.6 1.0 %rim.1 = (f32[19,16,4,128]{3,2,1,0:T(4,128)}, f32[3,512]{1,0:T(4,128)}) custom-call(f32[19,16,4,128]{3,2,1,0:T(4,128)} %bitcast.7, f32[19,2,4,128]{3,2,1,0:T(4,128)S(1)} %get-tuple-element.31.kept, f32[3,512]{1,0:T(4,128)S(1)} %get-tuple-element.32.part, f32[1216,128]{1,0:T(8,128)S(1)} %bitcast.5, ...), custom_call_target="tpu_custom_call", output_to_operand_aliasing={{0}: (0, {})} | custom-call | tf_op jit(solution)/shard_map/rim/pallas_call | solution.py:555
  (1 shorter events, 0.0 us)
Async XLA Ops:
  0.6 0.7 %copy-start.5 = (f32[3,512]{1,0:T(4,128)S(1)}, f32[3,512]{1,0:T(4,128)}, u32[]{:S(2)}) copy-start(f32[3,512]{1,0:T(4,128)} %frac.3) | copy-start | bytes 18436
  0.6 0.7 %copy-start.4 = (s32[3,512]{1,0:T(4,128)S(1)}, s32[3,512]{1,0:T(4,128)}, u32[]{:S(2)}) copy-start(s32[3,512]{1,0:T(4,128)} %base.3) | copy-start | bytes 18436
  0.7 0.8 %copy-start.1 = (f32[3,1536]{1,0:T(4,128)S(1)}, f32[3,1536]{1,0:T(4,128)}, u32[]{:S(2)}) copy-start(f32[3,1536]{1,0:T(4,128)} %rest.1) | copy-start | bytes 55300
  0.7 0.7 %copy-start.3 = (f32[1536]{0:T(1024)S(1)}, f32[1536]{0:T(1024)}, u32[]{:S(2)}) copy-start(f32[1536]{0:T(1024)} %param.10) | copy-start | bytes 18436
  0.7 0.7 %copy-start.2 = (s32[2,1536]{1,0:T(2,128)S(1)}, s32[2,1536]{1,0:T(2,128)}, u32[]{:S(2)}) copy-start(s32[2,1536]{1,0:T(2,128)} %edges.1) | copy-start | bytes 36868
  0.7 1.6 %copy-start = (f32[19,16,4,128]{3,2,1,0:T(4,128)S(1)}, f32[19,16,4,128]{3,2,1,0:T(4,128)}, u32[]{:S(2)}) copy-start(f32[19,16,4,128]{3,2,1,0:T(4,128)} %param.6) | copy-start | bytes 1867780
  2.4 7.3 %collective-permute-start = (f32[272,128]{1,0:T(8,128)S(1)}, f32[272,128]{1,0:T(8,128)S(1)}, u32[]{:S(2)}, u32[]{:S(2)}) collective-permute-start(f32[272,128]{1,0:T(8,128)S(1)} %get-tuple-element.24), channel_id=1, source_target_pairs={{0,1},{1,2},{2,3},{3,4},{4,5},{5,6},{6,7},{7,8},{8,9},{9,10},{10,1... | collective-permute-start | bytes 417800 | tf_op jit(solution)/shard_map/ppermute | solution.py:505
  5.4 10.3 %collective-permute-start.1 = (f32[272,128]{1,0:T(8,128)S(1)}, f32[272,128]{1,0:T(8,128)S(1)}, u32[]{:S(2)}, u32[]{:S(2)}) collective-permute-start(f32[272,128]{1,0:T(8,128)S(1)} %get-tuple-element.25), channel_id=1, source_target_pairs={{0,63},{1,0},{2,1},{3,2},{4,3},{5,4},{6,5},{7,6},{8,7},{9,8},{10,9... | collective-permute-start | bytes 417800 | tf_op jit(solution)/shard_map/ppermute | solution.py:505
  16.0 15.6 %collective-permute-start.2 = (f32[120,128]{1,0:T(8,128)S(1)}, f32[120,128]{1,0:T(8,128)S(1)}, u32[]{:S(2)}, u32[]{:S(2)}) collective-permute-start(f32[120,128]{1,0:T(8,128)S(1)} %get-tuple-element.33), channel_id=1, source_target_pairs={{0,64},{64,128},{128,192},{192,256},{256,320},{320,384},{384,448},... | collective-permute-start | bytes 184328 | tf_op jit(solution)/shard_map/ppermute | solution.py:505
  16.0 15.6 %collective-permute-start.3 = (f32[120,128]{1,0:T(8,128)S(1)}, f32[120,128]{1,0:T(8,128)S(1)}, u32[]{:S(2)}, u32[]{:S(2)}) collective-permute-start(f32[120,128]{1,0:T(8,128)S(1)} %get-tuple-element.34), channel_id=1, source_target_pairs={{0,960},{64,0},{128,64},{192,128},{256,192},{320,256},{384,320},{4... | collective-permute-start | bytes 184328 | tf_op jit(solution)/shard_map/ppermute | solution.py:505

commit v6 on v5

--- a/solution.py
+++ b/solution.py
@@ -280,7 +280,22 @@
         at += 4
 
 
-def merge_kernel(force_in, moment, edge, below, above, force, right, left):
+def merge_kernel(force, moment, edge, below, above, right, left, picked):
+    outgoing(right, force, moment, edge, below, above, (15, 16, 17), 15, None, 0, UP_X)
+    outgoing(left, force, moment, edge, below, above, (23, 0, 1), 0, 1, 24, DOWN_X)
+    picked[...] = jnp.zeros((24, NZ), f32)
+    for block, slab in ((below, 0), (above, 4)):
+        for n, x in enumerate((0, 1, 15)):
+            picked[3 * n : 3 * n + 3] = block[pl.ds(x, 3, stride=WX), :]
+        picked[9:18] = block[48:57]
+        wide = windows(picked[...], block[MARK_ROW : MARK_ROW + 1])
+        for c in range(3):
+            for n, (out, place) in enumerate(((left, 1), (left, 2), (right, 0), (right, 1), (right, 2), (left, 0))):
+                rows = pl.ds(21 * place + 3 * slab + c, 3, stride=3)
+                out[rows, :] = out[rows, :] + wide[3 * n : 3 * n + 3, c * NZ : (c + 1) * NZ]
+
+
+def whole_force(force, force_in, below, above):
     for row in range(0, SY * 3 * SX, SX):
         force[row : row + SX] = force_in[row : row + SX]
     for block, slab in ((below, 0), (above, 4)):
@@ -293,8 +308,6 @@
             for n, x in enumerate((16, 17, 23)):
                 rows = pl.ds((slab * 3 + c) * SX + x, 3, stride=3 * SX)
                 force[rows, :] = force[rows, :] + part[48 + 3 * n : 51 + 3 * n]
-    outgoing(right, force, moment, edge, below, above, (15, 16, 17), 15, None, 0, UP_X)
-    outgoing(left, force, moment, edge, below, above, (23, 0, 1), 0, 1, 24, DOWN_X)
 
 
 def collide(density, momentum, pull):
@@ -345,7 +358,10 @@
     return jnp.sum(value * plane, axis=0, keepdims=True)
 
 
-def inner_kernel(pop, force, moment, below, above, plane, z_high, z_low, fresh, kept, sampled, speed):
+def inner_kernel(
+    pop, force_in, moment, below, above, plane, z_high, z_low, fresh, kept, sampled, force, speed
+):
+    whole_force(force, force_in, below, above)
     left = 1.0 - 1.0 / relax_time
     for slab in range(SY):
         y_from = slab - 1
@@ -533,18 +549,23 @@
         [vert_base, vert_frac, lanes, marks],
         cost,
     )
-    force, right, left = call(
+    right, left = call(
         merge_kernel,
-        [((SY * 3 * SX, NZ), f32), ((SIDE_ROWS, NZ), f32), ((SIDE_ROWS, NZ), f32)],
-        [],
+        [((SIDE_ROWS, NZ), f32), ((SIDE_ROWS, NZ), f32)],
+        [pltpu.VMEM((24, NZ), f32)],
         "merge",
         [force, moment, edge, below, above],
     )
     west = shift(right, "gx", 1)
     east = shift(left, "gx", -1)
-    fresh, kept, part = call(
+    fresh, kept, part, force = call(
         inner_kernel,
-        [((19 * CELLS, NZ), f32), ((19, 2, WY, NZ), f32), ((3, VERTS), f32)],
+        [
+            ((19 * CELLS, NZ), f32),
+            ((19, 2, WY, NZ), f32),
+            ((3, VERTS), f32),
+            ((SY * 3 * SX, NZ), f32),
+        ],
         [pltpu.VMEM((3 * SY * WX, NZ), f32)],
         "inner",
         [pop, force, moment, below, above, inner_plane, z_high, z_low],

time: 32.8 us -> 32.8 us (level)
  no operation moved by 1% of the time
where the time goes in v6:
time: 32.8 us; the launch traced here: 32.6 us
  starting transfers between devices  19.5 us (59%)
  waiting for transfers between devices  7.61 us (23%)
  Pallas kernels  3.96 us (12%)
  between operations  0.75 us (2%)
  local copies, waits for them, and re-layouts  0.71 us (2%)
    ppermute x4, starting transfers between devices, shift(): lax.ppermute(value, axis, [(i, (i + step) % size) for i in range(size)])  19.5 us
    ppermute x4, waiting for transfers between devices, shift(): lax.ppermute(value, axis, [(i, (i + step) % size) for i in range(size)])  7.61 us
    pallas_call x6, Pallas kernels, call(): pl.pallas_call(kernel, out_shape=[jax.ShapeDtypeStruct(shape, kind) for s...  2.96 us
    pallas_call x1, Pallas kernels, per_device(): pl.pallas_call(rim_kernel, out_shape=[jax.ShapeDtypeStruct((19, WX, WY, N...  1.01 us
    unnamed x12, local copies, waits for them, and re-layouts  0.71 us
  transfers between devices with their start and end apart: 4, of which 3 were waited for; matrix products, arithmetic and copies ran while one was open for 0% of the time, Pallas kernels for 5%

profile of v6, /device:TPU:118, one launch (start us, length us, event | category | flops | bytes accessed | tf_op | source)
XLA Modules:
  0.0 32.6 jit_solution(7162507872316470453)
XLA Ops:
  0.6 0.0 copy-start.5
  0.6 0.0 copy-start.4
  0.7 0.0 copy-start.1
  0.7 0.0 copy-start.3
  0.7 0.0 copy-start.2
  0.7 0.0 copy-start
  0.7 0.6 %copy-done.5 = f32[3,512]{1,0:T(4,128)S(1)} copy-done((f32[3,512]{1,0:T(4,128)S(1)}, f32[3,512]{1,0:T(4,128)}, u32[]{:S(2)}) %copy-start.5) | copy-done | bytes 6168
  1.3 0.0 copy-done.4
  1.3 0.1 copy-done.1
  1.4 0.0 copy-done.3
  1.4 0.0 copy-done.2
  1.4 0.9 %spread.1 = (f32[168,128]{1,0:T(8,128)S(1)}, f32[8,128]{1,0:T(8,128)S(1)}, f32[112,512]{1,0:T(8,128)S(1)}, f32[48,512]{1,0:T(8,128)S(1)}) custom-call(s32[3,512]{1,0:T(4,128)S(1)} %copy-done.4, f32[3,512]{1,0:T(4,128)S(1)} %copy-done.5, s32[2,1536]{1,0:T(2,128)S(1)} %copy-done.2, f32[12,128]{1,0:T(8,128)S(1)} %bitcast.6, f32[3,1536]{1,0:T(4,128)S(1)} %copy-done.1, ...), custom_call_target="tpu_custom_call" | custom-call | tf_op jit(solution)/shard_map/spread/pallas_call | solution.py:507
  2.3 0.0 copy-done
  2.3 0.1 strips.1
  2.4 3.0 %collective-permute-start = (f32[272,128]{1,0:T(8,128)S(1)}, f32[272,128]{1,0:T(8,128)S(1)}, u32[]{:S(2)}, u32[]{:S(2)}) collective-permute-start(f32[272,128]{1,0:T(8,128)S(1)} %get-tuple-element.23), channel_id=1, source_target_pairs={{0,1},{1,2},{2,3},{3,4},{4,5},{5,6},{6,7},{7,8},{8,9},{9,10},{10,1... | collective-permute-start | bytes 417800 | tf_op jit(solution)/shard_map/ppermute | solution.py:521
  5.4 2.8 %collective-permute-start.1 = (f32[272,128]{1,0:T(8,128)S(1)}, f32[272,128]{1,0:T(8,128)S(1)}, u32[]{:S(2)}, u32[]{:S(2)}) collective-permute-start(f32[272,128]{1,0:T(8,128)S(1)} %get-tuple-element.24), channel_id=1, source_target_pairs={{0,63},{1,0},{2,1},{3,2},{4,3},{5,4},{6,5},{7,6},{8,7},{9,8},{10,9... | collective-permute-start | bytes 417800 | tf_op jit(solution)/shard_map/ppermute | solution.py:521
  8.2 0.4 %tables.1 = (f32[504,128]{1,0:T(8,128)S(1)}, bf16[128,512]{1,0:T(8,128)(2,1)S(1)}, bf16[128,512]{1,0:T(8,128)(2,1)S(1)}) custom-call(s32[3,512]{1,0:T(4,128)S(1)} %copy-done.4, f32[3,512]{1,0:T(4,128)S(1)} %copy-done.5, f32[168,128]{1,0:T(8,128)S(1)} %get-tuple-element.19.lanes, f32[8,128]{1,0:T(8,128)S(1)} %get-tuple-element.20.marks), custom_call_target="tpu_custom_call" | custom-call | flops 1073741824 | bytes 8388608 | tf_op jit(solution)/shard_map/tables/pallas_call | solution.py:507
  8.6 1.1 %collective-permute-done.below = f32[272,128]{1,0:T(8,128)S(1)} collective-permute-done((f32[272,128]{1,0:T(8,128)S(1)}, f32[272,128]{1,0:T(8,128)S(1)}, u32[]{:S(2)}, u32[]{:S(2)}) %collective-permute-start) | collective-permute-done | bytes 139296 | tf_op jit(solution)/shard_map/ppermute | solution.py:521
  9.7 6.1 %collective-permute-done.1.above = f32[272,128]{1,0:T(8,128)S(1)} collective-permute-done((f32[272,128]{1,0:T(8,128)S(1)}, f32[272,128]{1,0:T(8,128)S(1)}, u32[]{:S(2)}, u32[]{:S(2)}) %collective-permute-start.1) | collective-permute-done | bytes 139296 | tf_op jit(solution)/shard_map/ppermute | solution.py:521
  15.7 0.2 merge.1
  16.0 0.0 collective-permute-start.2
  16.0 13.7 %collective-permute-start.3 = (f32[120,128]{1,0:T(8,128)S(1)}, f32[120,128]{1,0:T(8,128)S(1)}, u32[]{:S(2)}, u32[]{:S(2)}) collective-permute-start(f32[120,128]{1,0:T(8,128)S(1)} %get-tuple-element.34), channel_id=1, source_target_pairs={{0,960},{64,0},{128,64},{192,128},{256,192},{320,256},{384,320},{4... | collective-permute-start | bytes 184328 | tf_op jit(solution)/shard_map/ppermute | solution.py:521
  29.7 1.4 %inner.1 = (f32[1216,128]{1,0:T(8,128)}, f32[19,2,4,128]{3,2,1,0:T(4,128)S(1)}, f32[3,512]{1,0:T(4,128)S(1)}, f32[504,128]{1,0:T(8,128)S(1)}) custom-call(f32[1216,128]{1,0:T(8,128)S(1)} %bitcast.4, f32[504,128]{1,0:T(8,128)S(1)} %get-tuple-element.21.force_in.force, f32[256,128]{1,0:T(8,128)S(1)} %get-tuple-element.22.moment, ...), custom_call_target="tpu_custom_call" | custom-call | flops 1073741824 | bytes 8388608 | tf_op jit(solution)/shard_map/inner/pallas_call | solution.py:507
  31.1 0.5 %collective-permute-done.2.west = f32[120,128]{1,0:T(8,128)S(1)} collective-permute-done((f32[120,128]{1,0:T(8,128)S(1)}, f32[120,128]{1,0:T(8,128)S(1)}, u32[]{:S(2)}, u32[]{:S(2)}) %collective-permute-start.2) | collective-permute-done | bytes 61472 | tf_op jit(solution)/shard_map/ppermute | solution.py:521
  31.6 0.0 collective-permute-done.3.east
  31.6 1.0 %rim.1 = (f32[19,16,4,128]{3,2,1,0:T(4,128)}, f32[3,512]{1,0:T(4,128)}) custom-call(f32[19,16,4,128]{3,2,1,0:T(4,128)} %bitcast.7, f32[19,2,4,128]{3,2,1,0:T(4,128)S(1)} %get-tuple-element.29.kept, f32[3,512]{1,0:T(4,128)S(1)} %get-tuple-element.30.part, f32[1216,128]{1,0:T(8,128)S(1)} %bitcast.5, ...), custom_call_target="tpu_custom_call", output_to_operand_aliasing={{0}: (0, {})} | custom-call | tf_op jit(solution)/shard_map/rim/pallas_call | solution.py:576
  (1 shorter events, 0.0 us)
Async XLA Ops:
  0.6 0.7 %copy-start.5 = (f32[3,512]{1,0:T(4,128)S(1)}, f32[3,512]{1,0:T(4,128)}, u32[]{:S(2)}) copy-start(f32[3,512]{1,0:T(4,128)} %frac.3) | copy-start | bytes 18436
  0.6 0.7 %copy-start.4 = (s32[3,512]{1,0:T(4,128)S(1)}, s32[3,512]{1,0:T(4,128)}, u32[]{:S(2)}) copy-start(s32[3,512]{1,0:T(4,128)} %base.3) | copy-start | bytes 18436
  0.7 0.8 %copy-start.1 = (f32[3,1536]{1,0:T(4,128)S(1)}, f32[3,1536]{1,0:T(4,128)}, u32[]{:S(2)}) copy-start(f32[3,1536]{1,0:T(4,128)} %rest.1) | copy-start | bytes 55300
  0.7 0.7 %copy-start.3 = (f32[1536]{0:T(1024)S(1)}, f32[1536]{0:T(1024)}, u32[]{:S(2)}) copy-start(f32[1536]{0:T(1024)} %param.10) | copy-start | bytes 18436
  0.7 0.7 %copy-start.2 = (s32[2,1536]{1,0:T(2,128)S(1)}, s32[2,1536]{1,0:T(2,128)}, u32[]{:S(2)}) copy-start(s32[2,1536]{1,0:T(2,128)} %edges.1) | copy-start | bytes 36868
  0.7 1.6 %copy-start = (f32[19,16,4,128]{3,2,1,0:T(4,128)S(1)}, f32[19,16,4,128]{3,2,1,0:T(4,128)}, u32[]{:S(2)}) copy-start(f32[19,16,4,128]{3,2,1,0:T(4,128)} %param.6) | copy-start | bytes 1867780
  2.4 7.3 %collective-permute-start = (f32[272,128]{1,0:T(8,128)S(1)}, f32[272,128]{1,0:T(8,128)S(1)}, u32[]{:S(2)}, u32[]{:S(2)}) collective-permute-start(f32[272,128]{1,0:T(8,128)S(1)} %get-tuple-element.23), channel_id=1, source_target_pairs={{0,1},{1,2},{2,3},{3,4},{4,5},{5,6},{6,7},{7,8},{8,9},{9,10},{10,1... | collective-permute-start | bytes 417800 | tf_op jit(solution)/shard_map/ppermute | solution.py:521
  5.4 10.3 %collective-permute-start.1 = (f32[272,128]{1,0:T(8,128)S(1)}, f32[272,128]{1,0:T(8,128)S(1)}, u32[]{:S(2)}, u32[]{:S(2)}) collective-permute-start(f32[272,128]{1,0:T(8,128)S(1)} %get-tuple-element.24), channel_id=1, source_target_pairs={{0,63},{1,0},{2,1},{3,2},{4,3},{5,4},{6,5},{7,6},{8,7},{9,8},{10,9... | collective-permute-start | bytes 417800 | tf_op jit(solution)/shard_map/ppermute | solution.py:521
  16.0 15.6 %collective-permute-start.2 = (f32[120,128]{1,0:T(8,128)S(1)}, f32[120,128]{1,0:T(8,128)S(1)}, u32[]{:S(2)}, u32[]{:S(2)}) collective-permute-start(f32[120,128]{1,0:T(8,128)S(1)} %get-tuple-element.33), channel_id=1, source_target_pairs={{0,64},{64,128},{128,192},{192,256},{256,320},{320,384},{384,448},... | collective-permute-start | bytes 184328 | tf_op jit(solution)/shard_map/ppermute | solution.py:521
  16.0 15.6 %collective-permute-start.3 = (f32[120,128]{1,0:T(8,128)S(1)}, f32[120,128]{1,0:T(8,128)S(1)}, u32[]{:S(2)}, u32[]{:S(2)}) collective-permute-start(f32[120,128]{1,0:T(8,128)S(1)} %get-tuple-element.34), channel_id=1, source_target_pairs={{0,960},{64,0},{128,64},{192,128},{256,192},{320,256},{384,320},{4... | collective-permute-start | bytes 184328 | tf_op jit(solution)/shard_map/ppermute | solution.py:521
